TPU v7x, 32 devices: a whole 2x2x4 slice. The times are simulated.
32 devices in a mesh: clips: 2 (over y), video: 4 (over z), audio: 4 (over x, core).
Axes of the slice: x: 2, y: 2, z: 4, core: 2. Of those that a mesh axis runs over, the one named last changes fastest.
Arguments:
- video_q: bfloat16 [5120, 1536], P(('clips', 'video', 'audio')), parts along dimension 0, may hold values from -130 to 130
- video_k: bfloat16 [5120, 1536], P(('clips', 'video', 'audio')), parts along dimension 0, may hold values from -130 to 130
- video_v: bfloat16 [5120, 1536], P(('clips', 'video', 'audio')), parts along dimension 0, may hold values from -6 to 6
- audio_q: bfloat16 [512, 1536], P(('clips', 'video', 'audio')), parts along dimension 0, may hold values from -130 to 130
- audio_k: bfloat16 [512, 1536], P(('clips', 'video', 'audio')), parts along dimension 0, may hold values from -130 to 130
- audio_v: bfloat16 [512, 1536], P(('clips', 'video', 'audio')), parts along dimension 0, may hold values from -6 to 6
- norm_gain: float32 [4, 1536], replicated, may hold values from 0.49 to 6
- video_dout: bfloat16 [5120, 1536], P(('clips', 'video', 'audio')), parts along dimension 0, may hold values from -6 to 6
- audio_dout: bfloat16 [512, 1536], P(('clips', 'video', 'audio')), parts along dimension 0, may hold values from -6 to 6
- link: int32 [32, 5], P(('clips', 'video', 'audio')), parts along dimension 0, may hold values from 0 to 1, as said below
Outputs:
- video_out: bfloat16 [5120, 1536], P(('clips', 'video', 'audio')), parts along dimension 0
- audio_out: bfloat16 [512, 1536], P(('clips', 'video', 'audio')), parts along dimension 0
- grad_video_q: bfloat16 [5120, 1536], P(('clips', 'video', 'audio')), parts along dimension 0
- grad_video_k: bfloat16 [5120, 1536], P(('clips', 'video', 'audio')), parts along dimension 0
- grad_video_v: bfloat16 [5120, 1536], P(('clips', 'video', 'audio')), parts along dimension 0
- grad_audio_q: bfloat16 [512, 1536], P(('clips', 'video', 'audio')), parts along dimension 0
- grad_audio_k: bfloat16 [512, 1536], P(('clips', 'video', 'audio')), parts along dimension 0
- grad_audio_v: bfloat16 [512, 1536], P(('clips', 'video', 'audio')), parts along dimension 0
There are 2 independent parts, one for each index of `clips`. A program takes and returns all parts, laid end to end along the dimension named above; an argument that names none is the same for every part. Nothing has to cross between parts.
Inputs may be any that keep to these rules, and one draw needn't show every extreme that they name: `link`: row b, column j links video block b with audio block b + j - 2; column 2 is 1 in every row, the ones of a row are consecutive, and columns that name an audio block outside 0 to 15 are 0.
All inputs are finite; a program needn't handle non-finite values.
Results may differ from a plain program's by a relative error of at most 0.038.
The roundings to bfloat16 on the way count: a program that leaves them out, or rounds other values in their place, can miss the bound.
Values may be sent and summed in bfloat16 or wider, within the bound.
A program may use at most 64 MiB of HBM per device.

v0:
```python
import math

import jax
import jax.numpy as jnp
from jax import lax
from jax.sharding import PartitionSpec as P

DH = 128
FRAME = 960
AFRAME = 96
R = 2
SPAN = 5


EPSILON = 1e-06
HUGE = 1e30


def passed_along(block, axis, distance):
    devices = range(lax.axis_size(axis))
    route = [(i - distance, i) for i in devices if i - distance in devices]
    return lax.ppermute(block, axis, route)


def prepare(values, gain_row, places):
    row_count = values.shape[0]
    head_count = values.shape[1] // DH
    half_size = DH // 2
    shaped = values.reshape(row_count, head_count, DH)
    scaled = shaped * lax.rsqrt(jnp.mean(shaped * shaped, axis=-1, keepdims=True) + EPSILON)
    normed = scaled * gain_row.reshape(head_count, DH)
    inverse = jnp.exp(jnp.arange(half_size).astype(jnp.float32) * (-2.0 * math.log(10000.0) / DH))
    angles = places[:, None] * inverse[None, :]
    cosine = jnp.cos(angles)[:, None, :]
    sine_part = jnp.sin(angles)[:, None, :]
    first_half = normed[:, :, :half_size]
    second_half = normed[:, :, half_size:]
    turned = jnp.concatenate(
        [
            first_half * cosine - second_half * sine_part,
            second_half * cosine + first_half * sine_part,
        ],
        axis=-1,
    )
    return turned.reshape(row_count, head_count * DH)


def on_device(
    video_q, video_k, video_v, audio_q, audio_k, audio_v, norm_gain, video_dout, audio_dout, link
):
    video_rows = video_q.shape[0]
    audio_rows = audio_q.shape[0]
    channels = video_q.shape[1]
    head_count = channels // DH
    attn_scale = DH ** (-0.5)
    device_index = lax.axis_index(("video", "audio"))
    video_places = (
        (device_index * video_rows + jnp.arange(video_rows, dtype=jnp.int32)) // FRAME
    ).astype(jnp.float32)
    audio_places = (device_index * audio_rows + jnp.arange(audio_rows, dtype=jnp.int32)).astype(
        jnp.float32
    ) / AFRAME
    query_video, query_video_back = jax.vjp(
        lambda values: prepare(values, norm_gain[0], video_places), video_q.astype(jnp.float32)
    )
    key_video, key_video_back = jax.vjp(
        lambda values: prepare(values, norm_gain[1], video_places), video_k.astype(jnp.float32)
    )
    query_audio, query_audio_back = jax.vjp(
        lambda values: prepare(values, norm_gain[2], audio_places), audio_q.astype(jnp.float32)
    )
    key_audio, key_audio_back = jax.vjp(
        lambda values: prepare(values, norm_gain[3], audio_places), audio_k.astype(jnp.float32)
    )
    video_shape = (video_rows, head_count, DH)
    audio_shape = (audio_rows, head_count, DH)
    window_shape = (SPAN * audio_rows, head_count, DH)
    video_qr = query_video.astype(jnp.bfloat16).reshape(video_shape)
    video_kr = key_video.astype(jnp.bfloat16).reshape(video_shape)
    video_vr = video_v.reshape(video_shape)
    audio_qr = query_audio.astype(jnp.bfloat16)
    audio_kr = key_audio.astype(jnp.bfloat16)
    linked = link[0] > 0
    keep_rows = jnp.repeat(linked, audio_rows)
    own_audio = (audio_qr, audio_kr, audio_v)
    slot_pieces = []
    for slot_index in range(SPAN):
        if slot_index == R:
            slot_pieces.append(own_audio)
        else:
            slot_pieces.append(
                passed_along(
                    (own_audio[0], own_audio[1], own_audio[2]), ("video", "audio"), R - slot_index
                )
            )
    window_audio = tuple(
        (
            jnp.concatenate([arrival[member] for arrival in slot_pieces], axis=0)
            for member in range(3)
        )
    )
    query_win = window_audio[0].reshape(window_shape)
    key_win = window_audio[1].reshape(window_shape)
    value_win = window_audio[2].reshape(window_shape)
    scores_video = (
        jnp.einsum("qhd,khd->hqk", video_qr, key_win, preferred_element_type=jnp.float32)
        * attn_scale
    )
    masked_video = jnp.where(keep_rows[None, None, :], scores_video, -HUGE)
    top_video = jnp.max(masked_video, axis=-1)
    weights_video = jnp.exp(masked_video - top_video[:, :, None])
    total_video = jnp.sum(weights_video, axis=-1)
    mixed_video = jnp.einsum(
        "hqk,khd->qhd",
        weights_video.astype(jnp.bfloat16),
        value_win,
        preferred_element_type=jnp.float32,
    )
    video_out = (mixed_video / total_video.T[:, :, None]).astype(jnp.bfloat16)
    lse_video = top_video + jnp.log(total_video)

    def partial_slot(query_rows):
        scores_slot = (
            jnp.einsum("ahd,khd->hak", query_rows, video_kr, preferred_element_type=jnp.float32)
            * attn_scale
        )
        top_slot = jnp.max(scores_slot, axis=-1)
        weights_slot = jnp.exp(scores_slot - top_slot[:, :, None])
        total_slot = jnp.sum(weights_slot, axis=-1)
        mixed_slot = jnp.einsum(
            "hak,khd->ahd",
            weights_slot.astype(jnp.bfloat16),
            video_vr,
            preferred_element_type=jnp.float32,
        )
        return (mixed_slot.astype(jnp.bfloat16), top_slot.T, total_slot.T, scores_slot)

    def skipped_slot(query_rows):
        return (
            jnp.zeros(audio_shape, jnp.bfloat16),
            jnp.zeros((audio_rows, head_count), jnp.float32),
            jnp.zeros((audio_rows, head_count), jnp.float32),
            jnp.zeros((head_count, audio_rows, video_rows), jnp.float32),
        )

    partials = []
    for slot_index in range(SPAN):
        rows_here = query_win[slot_index * audio_rows : (slot_index + 1) * audio_rows]
        partials.append(lax.cond(linked[slot_index], partial_slot, skipped_slot, rows_here))
    received = []
    for slot_index in range(SPAN):
        mixed_here = partials[slot_index][0].reshape(audio_rows, channels)
        if slot_index == R:
            received.append((mixed_here, partials[slot_index][1], partials[slot_index][2]))
        else:
            mixed_back = passed_along(mixed_here, ("video", "audio"), slot_index - R)
            stats_back = passed_along(
                (partials[slot_index][1], partials[slot_index][2]),
                ("video", "audio"),
                slot_index - R,
            )
            received.append((mixed_back, stats_back[0], stats_back[1]))
    stack_mixed = jnp.stack([arrival[0].reshape(audio_shape) for arrival in received])
    stack_top = jnp.stack([arrival[1] for arrival in received])
    stack_total = jnp.stack([arrival[2] for arrival in received])
    valid_parts = stack_total > 0.0
    lifted = jnp.where(valid_parts, stack_top, -HUGE)
    best_top = jnp.max(lifted, axis=0)
    factors = jnp.where(valid_parts, jnp.exp(lifted - best_top[None]), 0.0)
    total_audio = jnp.sum(factors * stack_total, axis=0)
    combined = (
        jnp.sum(factors[..., None] * stack_mixed.astype(jnp.float32), axis=0)
        / total_audio[..., None]
    )
    audio_out = combined.astype(jnp.bfloat16)
    lse_audio = best_top + jnp.log(total_audio)
    grad_audio_rows = audio_dout.reshape(audio_shape)
    delta_audio = jnp.sum(
        grad_audio_rows.astype(jnp.float32) * audio_out.astype(jnp.float32), axis=-1
    )
    grad_video_rows = video_dout.reshape(video_shape)
    probs_video = jnp.exp(masked_video - lse_video[:, :, None])
    dvalue_win = jnp.einsum(
        "hqk,qhd->khd",
        probs_video.astype(jnp.bfloat16),
        grad_video_rows,
        preferred_element_type=jnp.float32,
    ).astype(jnp.bfloat16)
    dprob_video = jnp.einsum(
        "qhd,khd->hqk", grad_video_rows, value_win, preferred_element_type=jnp.float32
    )
    delta_video = jnp.sum(
        grad_video_rows.astype(jnp.float32) * video_out.astype(jnp.float32), axis=-1
    ).T
    dscore_video = (probs_video * (dprob_video - delta_video[:, :, None])).astype(jnp.bfloat16)
    dquery_video = (
        jnp.einsum("hqk,khd->qhd", dscore_video, key_win, preferred_element_type=jnp.float32)
        * attn_scale
    )
    dkey_win = (
        jnp.einsum("hqk,qhd->khd", dscore_video, video_qr, preferred_element_type=jnp.float32)
        * attn_scale
    ).astype(jnp.bfloat16)
    dkey_flat = dkey_win.reshape(SPAN * audio_rows, channels)
    dvalue_flat = dvalue_win.reshape(SPAN * audio_rows, channels)
    grad_pieces = []
    stat_pieces = []
    for slot_index in range(SPAN):
        if slot_index == R:
            grad_pieces.append(audio_dout)
            stat_pieces.append((lse_audio, delta_audio))
        else:
            grad_pieces.append(passed_along(audio_dout, ("video", "audio"), R - slot_index))
            stat_pieces.append(
                passed_along((lse_audio, delta_audio), ("video", "audio"), R - slot_index)
            )
    grad_win = jnp.concatenate(grad_pieces, axis=0)
    lse_win = jnp.concatenate([arrival[0] for arrival in stat_pieces], axis=0)
    delta_win = jnp.concatenate([arrival[1] for arrival in stat_pieces], axis=0)
    grad_win = grad_win.reshape(window_shape)

    def grad_slot(query_rows, scores_slot, grad_rows, lse_rows, delta_rows, row_keep):
        probs_slot = jnp.where(
            row_keep[None, :, None], jnp.exp(scores_slot - lse_rows.T[:, :, None]), 0.0
        )
        dvalue_slot = jnp.einsum(
            "hak,ahd->khd",
            probs_slot.astype(jnp.bfloat16),
            grad_rows,
            preferred_element_type=jnp.float32,
        )
        dprob_slot = jnp.einsum(
            "ahd,khd->hak", grad_rows, video_vr, preferred_element_type=jnp.float32
        )
        dscore_slot = (probs_slot * (dprob_slot - delta_rows.T[:, :, None])).astype(jnp.bfloat16)
        dkey_slot = (
            jnp.einsum("hak,ahd->khd", dscore_slot, query_rows, preferred_element_type=jnp.float32)
            * attn_scale
        )
        dquery_slot = (
            jnp.einsum("hak,khd->ahd", dscore_slot, video_kr, preferred_element_type=jnp.float32)
            * attn_scale
        ).astype(jnp.bfloat16)
        return (dkey_slot, dvalue_slot, dquery_slot)

    all_rows = jnp.ones((audio_rows,), jnp.bool_)

    def run_slot(operands):
        return grad_slot(operands[0], operands[1], operands[2], operands[3], operands[4], all_rows)

    def skipped_grads(operands):
        return (
            jnp.zeros(video_shape, jnp.float32),
            jnp.zeros(video_shape, jnp.float32),
            jnp.zeros(audio_shape, jnp.bfloat16),
        )

    dkey_video = jnp.zeros(video_shape, jnp.float32)
    dvalue_video = jnp.zeros(video_shape, jnp.float32)
    dquery_slots = []
    for slot_index in range(SPAN):
        slot_start = slot_index * audio_rows
        slot_end = slot_start + audio_rows
        operands = (
            query_win[slot_start:slot_end],
            partials[slot_index][3],
            grad_win[slot_start:slot_end],
            lse_win[slot_start:slot_end],
            delta_win[slot_start:slot_end],
        )
        dkey_slot, dvalue_slot, dquery_slot = lax.cond(
            linked[slot_index], run_slot, skipped_grads, operands
        )
        dkey_video = dkey_video + dkey_slot
        dvalue_video = dvalue_video + dvalue_slot
        dquery_slots.append(dquery_slot.reshape(audio_rows, channels))
    audio_terms = []
    for slot_index in range(SPAN):
        slot_start = slot_index * audio_rows
        key_here = dkey_flat[slot_start : slot_start + audio_rows]
        value_here = dvalue_flat[slot_start : slot_start + audio_rows]
        if slot_index == R:
            audio_terms.append((dquery_slots[slot_index], key_here, value_here))
        else:
            audio_terms.append(
                passed_along(
                    (dquery_slots[slot_index], key_here, value_here),
                    ("video", "audio"),
                    slot_index - R,
                )
            )
    dquery_audio = jnp.sum(
        jnp.stack([arrival[0] for arrival in audio_terms]).astype(jnp.float32), axis=0
    )
    dkey_audio = jnp.sum(
        jnp.stack([arrival[1] for arrival in audio_terms]).astype(jnp.float32), axis=0
    )
    dvalue_audio = jnp.sum(
        jnp.stack([arrival[2] for arrival in audio_terms]).astype(jnp.float32), axis=0
    )
    grad_video_q = query_video_back(dquery_video.reshape(video_rows, channels))[0].astype(
        jnp.bfloat16
    )
    grad_video_k = key_video_back(dkey_video.reshape(video_rows, channels))[0].astype(jnp.bfloat16)
    grad_video_v = dvalue_video.reshape(video_rows, channels).astype(jnp.bfloat16)
    grad_audio_q = query_audio_back(dquery_audio)[0].astype(jnp.bfloat16)
    grad_audio_k = key_audio_back(dkey_audio)[0].astype(jnp.bfloat16)
    grad_audio_v = dvalue_audio.astype(jnp.bfloat16)
    return (
        video_out.reshape(video_rows, channels),
        audio_out.reshape(audio_rows, channels),
        grad_video_q,
        grad_video_k,
        grad_video_v,
        grad_audio_q,
        grad_audio_k,
        grad_audio_v,
    )


def solution(mesh):
    return jax.shard_map(
        on_device,
        mesh=mesh,
        in_specs=(
            P(("clips", "video", "audio"), None),
            P(("clips", "video", "audio"), None),
            P(("clips", "video", "audio"), None),
            P(("clips", "video", "audio"), None),
            P(("clips", "video", "audio"), None),
            P(("clips", "video", "audio"), None),
            P(),
            P(("clips", "video", "audio"), None),
            P(("clips", "video", "audio"), None),
            P(("clips", "video", "audio"), None),
        ),
        out_specs=(
            P(("clips", "video", "audio"), None),
            P(("clips", "video", "audio"), None),
            P(("clips", "video", "audio"), None),
            P(("clips", "video", "audio"), None),
            P(("clips", "video", "audio"), None),
            P(("clips", "video", "audio"), None),
            P(("clips", "video", "audio"), None),
            P(("clips", "video", "audio"), None),
        ),
        check_vma=False,
    )
```

profile of v0, /device:TPU:20, one launch (start us, length us, event | category | flops | bytes accessed | tf_op | source)
XLA Modules:
  0.0 291.4 jit_solution(2648130857315181858)
XLA Ops:
  0.7 2.9 collective-permute-start.2
  3.5 1.9 collective-permute-start.1
  5.5 3.1 %collective-permute-start = (bf16[16,1536]{1,0:T(8,128)(2,1)}, bf16[16,1536]{1,0:T(8,128)(2,1)}, u32[]{:S(2)}, u32[]{:S(2)}) collective-permute-start(bf16[16,1536]{1,0:T(8,128)(2,1)} %param.35), channel_id=1, source_target_pairs={{0,2},{1,3},{2,4},{3,5},{4,6},{5,7},{6,8},{7,9},{8,10},{9,11},{10,... | collective-permute-start | bytes 147464 | tf_op jit(solution)/shard_map/ppermute | solution.py:22
  8.6 3.7 %collective-permute-start.3 = (bf16[16,1536]{1,0:T(8,128)(2,1)}, bf16[16,1536]{1,0:T(8,128)(2,1)}, u32[]{:S(2)}, u32[]{:S(2)}) collective-permute-start(bf16[16,1536]{1,0:T(8,128)(2,1)} %param.35), channel_id=1, source_target_pairs={{2,0},{3,1},{4,2},{5,3},{6,4},{7,5},{8,6},{9,7},{10,8},{11,9},{12,... | collective-permute-start | bytes 147464 | tf_op jit(solution)/shard_map/ppermute | solution.py:22
  15.4 2.2 collective-permute-start.4
  30.3 4.0 %conditional.12 = (f32[12,16,160]{2,1,0:T(8,128)}, f32[1,16,12]{1,2,0:T(8,128)}, f32[1,16,12]{1,2,0:T(8,128)S(1)}, bf16[1,16,12,128]{3,2,1,0:T(8,128)(2,1)S(1)}) conditional(s32[]{:T(128)} %bitcast.50, () %tuple.112, (bf16[16,12,128]{2,1,0:T(8,128)(2,1)S(1)}, bf16[160,12,128]{2,0,1:T(8,128)(2,1)S(1)}, bf16[160,12,128]{2,1,0:T(8,128)(2,1)S(1)}) %tuple.113), branch_computations={%region_14.15_spmd, %region_15.18_spmd} | conditional | flops 15937152 | bytes 1551392 | solution.py:149
  34.4 3.0 %collective-permute-start.5 = (bf16[16,1536]{1,0:T(8,128)(2,1)}, bf16[16,1536]{1,0:T(8,128)(2,1)S(1)}, u32[]{:S(2)}, u32[]{:S(2)}) collective-permute-start(bf16[16,1536]{1,0:T(8,128)(2,1)} %bitcast.401), channel_id=1, source_target_pairs={{0,1},{1,2},{2,3},{3,4},{4,5},{5,6},{6,7},{7,8},{8,9},{9,10},{10,1... | collective-permute-start | bytes 147464 | tf_op jit(solution)/shard_map/ppermute | solution.py:22
  38.3 2.7 collective-permute-done.5
  44.9 3.6 %collective-permute-start.7 = (bf16[16,1536]{1,0:T(8,128)(2,1)}, bf16[16,1536]{1,0:T(8,128)(2,1)S(1)}, u32[]{:S(2)}, u32[]{:S(2)}) collective-permute-start(bf16[16,1536]{1,0:T(8,128)(2,1)} %bitcast.401), channel_id=1, source_target_pairs={{2,0},{3,1},{4,2},{5,3},{6,4},{7,5},{8,6},{9,7},{10,8},{11,9},{12,... | collective-permute-start | bytes 147464 | tf_op jit(solution)/shard_map/ppermute | solution.py:22
  48.6 2.5 collective-permute-done.7
  51.1 3.3 %collective-permute-start.28 = (bf16[16,1536]{1,0:T(8,128)(2,1)}, bf16[16,1536]{1,0:T(8,128)(2,1)S(1)}, u32[]{:S(2)}, u32[]{:S(2)}) collective-permute-start(bf16[16,1536]{1,0:T(8,128)(2,1)} %param.38), channel_id=1, source_target_pairs={{0,1},{1,2},{2,3},{3,4},{4,5},{5,6},{6,7},{7,8},{8,9},{9,10},{10,1... | collective-permute-start | bytes 147464 | tf_op jit(solution)/shard_map/ppermute | solution.py:22
  56.8 3.6 %collective-permute-start.14 = (bf16[16,1536]{1,0:T(8,128)(2,1)}, bf16[16,1536]{1,0:T(8,128)(2,1)}, u32[]{:S(2)}, u32[]{:S(2)}) collective-permute-start(bf16[16,1536]{1,0:T(8,128)(2,1)} %bitcast.400), channel_id=1, source_target_pairs={{2,0},{3,1},{4,2},{5,3},{6,4},{7,5},{8,6},{9,7},{10,8},{11,9},{12,... | collective-permute-start | bytes 147464 | tf_op jit(solution)/shard_map/ppermute | solution.py:22
  61.3 3.2 %collective-permute-start.12 = (bf16[16,1536]{1,0:T(8,128)(2,1)}, bf16[16,1536]{1,0:T(8,128)(2,1)}, u32[]{:S(2)}, u32[]{:S(2)}) collective-permute-start(bf16[16,1536]{1,0:T(8,128)(2,1)} %bitcast.400), channel_id=1, source_target_pairs={{1,0},{2,1},{3,2},{4,3},{5,4},{6,5},{7,6},{8,7},{9,8},{10,9},{11,1... | collective-permute-start | bytes 147464 | tf_op jit(solution)/shard_map/ppermute | solution.py:22
  65.3 1.9 collective-permute-start.10
  68.1 2.1 collective-permute-start.8
  82.4 4.6 %collective-permute-start.9 = (f32[16,12]{0,1:T(8,128)}, f32[16,12]{0,1:T(8,128)}, u32[]{:S(2)}, u32[]{:S(2)}) collective-permute-start(f32[16,12]{0,1:T(8,128)} %get-tuple-element.231), channel_id=1, source_target_pairs={{2,0},{3,1},{4,2},{5,3},{6,4},{7,5},{8,6},{9,7},{10,8},{11,9},{12,... | collective-permute-start | bytes 2312 | tf_op jit(solution)/shard_map/ppermute | solution.py:22
  87.0 1.9 collective-permute-start.16
  89.6 3.8 %collective-permute-start.20 = (bf16[16,1536]{1,0:T(8,128)(2,1)}, bf16[16,1536]{1,0:T(8,128)(2,1)}, u32[]{:S(2)}, u32[]{:S(2)}) collective-permute-start(bf16[16,1536]{1,0:T(8,128)(2,1)} %copy_bitcast_fusion.24), channel_id=1, source_target_pairs={{2,0},{3,1},{4,2},{5,3},{6,4},{7,5},{8,6},{9,7},{10,8},{11,9},{12,... | collective-permute-start | bytes 147464 | tf_op jit(solution)/shard_map/ppermute | solution.py:22
  95.3 4.7 %collective-permute-start.11 = (f32[16,12]{0,1:T(8,128)}, f32[16,12]{0,1:T(8,128)}, u32[]{:S(2)}, u32[]{:S(2)}) collective-permute-start(f32[16,12]{0,1:T(8,128)} %get-tuple-element.232), channel_id=1, source_target_pairs={{1,0},{2,1},{3,2},{4,3},{5,4},{6,5},{7,6},{8,7},{9,8},{10,9},{11,1... | collective-permute-start | bytes 2312 | tf_op jit(solution)/shard_map/ppermute | solution.py:22
  102.6 2.5 conditional.14
  118.1 12.1 %collective-permute-start.21 = (bf16[16,1536]{1,0:T(8,128)(2,1)}, bf16[16,1536]{1,0:T(8,128)(2,1)}, u32[]{:S(2)}, u32[]{:S(2)}) collective-permute-start(bf16[16,1536]{1,0:T(8,128)(2,1)} %copy_bitcast_fusion.23), channel_id=1, source_target_pairs={{1,0},{2,1},{3,2},{4,3},{5,4},{6,5},{7,6},{8,7},{9,8},{10,9},{11,1... | collective-permute-start | bytes 147464 | tf_op jit(solution)/shard_map/ppermute | solution.py:22
  136.9 2.7 collective-permute-start.15
  139.7 3.9 %collective-permute-done.15 = f32[16,12]{0,1:T(8,128)S(1)} collective-permute-done((f32[16,12]{0,1:T(8,128)}, f32[16,12]{0,1:T(8,128)S(1)}, u32[]{:S(2)}, u32[]{:S(2)}) %collective-permute-start.15) | collective-permute-done | bytes 800 | tf_op jit(solution)/shard_map/ppermute | solution.py:22
  148.2 4.7 %collective-permute-done.19 = f32[16,12]{0,1:T(8,128)S(1)} collective-permute-done((f32[16,12]{0,1:T(8,128)}, f32[16,12]{0,1:T(8,128)S(1)}, u32[]{:S(2)}, u32[]{:S(2)}) %collective-permute-start.19) | collective-permute-done | bytes 800 | tf_op jit(solution)/shard_map/ppermute | solution.py:22
  158.2 4.8 %collective-permute-start.40 = (bf16[16,1536]{1,0:T(8,128)(2,1)}, bf16[16,1536]{1,0:T(8,128)(2,1)}, u32[]{:S(2)}, u32[]{:S(2)}) collective-permute-start(bf16[16,1536]{1,0:T(8,128)(2,1)} %bitcast.441), channel_id=1, source_target_pairs={{2,0},{3,1},{4,2},{5,3},{6,4},{7,5},{8,6},{9,7},{10,8},{11,9},{12,... | collective-permute-start | bytes 147464 | tf_op jit(solution)/shard_map/ppermute | solution.py:22
  167.3 2.9 %collective-permute-start.41 = (bf16[16,1536]{1,0:T(8,128)(2,1)}, bf16[16,1536]{1,0:T(8,128)(2,1)S(1)}, u32[]{:S(2)}, u32[]{:S(2)}) collective-permute-start(bf16[16,1536]{1,0:T(8,128)(2,1)} %bitcast.440), channel_id=1, source_target_pairs={{1,0},{2,1},{3,2},{4,3},{5,4},{6,5},{7,6},{8,7},{9,8},{10,9},{11,1... | collective-permute-start | bytes 147464 | tf_op jit(solution)/shard_map/ppermute | solution.py:22
  172.3 2.9 collective-permute-start.46
  178.8 2.8 collective-permute-start.47
  183.1 1.9 collective-permute-start.42
  186.5 3.2 %collective-permute-done.42 = bf16[16,1536]{1,0:T(8,128)(2,1)} collective-permute-done((bf16[16,1536]{1,0:T(8,128)(2,1)}, bf16[16,1536]{1,0:T(8,128)(2,1)}, u32[]{:S(2)}, u32[]{:S(2)}) %collective-permute-start.42) | collective-permute-done | bytes 49184 | tf_op jit(solution)/shard_map/ppermute | solution.py:22
  189.7 3.5 %collective-permute-start.43 = (bf16[16,1536]{1,0:T(8,128)(2,1)}, bf16[16,1536]{1,0:T(8,128)(2,1)S(1)}, u32[]{:S(2)}, u32[]{:S(2)}) collective-permute-start(bf16[16,1536]{1,0:T(8,128)(2,1)} %bitcast.438), channel_id=1, source_target_pairs={{0,2},{1,3},{2,4},{3,5},{4,6},{5,7},{6,8},{7,9},{8,10},{9,11},{10,... | collective-permute-start | bytes 147464 | tf_op jit(solution)/shard_map/ppermute | solution.py:22
  200.8 2.6 collective-permute-start.25
  203.5 4.1 %collective-permute-start.34 = (bf16[16,1536]{1,0:T(8,128)(2,1)}, bf16[16,1536]{1,0:T(8,128)(2,1)}, u32[]{:S(2)}, u32[]{:S(2)}) collective-permute-start(bf16[16,1536]{1,0:T(8,128)(2,1)} %param.38), channel_id=1, source_target_pairs={{2,0},{3,1},{4,2},{5,3},{6,4},{7,5},{8,6},{9,7},{10,8},{11,9},{12,... | collective-permute-start | bytes 147464 | tf_op jit(solution)/shard_map/ppermute | solution.py:22
  207.6 2.0 collective-permute-start.24
  209.6 4.8 %collective-permute-start.26 = (f32[16,12]{1,0:T(8,128)}, f32[16,12]{1,0:T(8,128)}, u32[]{:S(2)}, u32[]{:S(2)}) collective-permute-start(f32[16,12]{1,0:T(8,128)} %get-tuple-element.471), channel_id=1, source_target_pairs={{0,2},{1,3},{2,4},{3,5},{4,6},{5,7},{6,8},{7,9},{8,10},{9,11},{10,... | collective-permute-start | bytes 2312 | tf_op jit(solution)/shard_map/ppermute | solution.py:22
  219.1 8.3 %conditional.17 = (f32[160,12,128]{2,0,1:T(8,128)S(1)}, f32[160,12,128]{2,0,1:T(8,128)S(1)}, bf16[1,16,1536]{2,1,0:T(8,128)(2,1)}) conditional(s32[]{:T(128)} %bitcast.50, () %tuple.122, (f32[16,12]{0,1:T(8,128)}, f32[12,16,160]{2,1,0:T(8,128)}, bf16[16,12,128]{2,1,0:T(8,128)(2,1)}, bf16[160,12,128]{2,1,0:T(8,128)(2,1)S(1)}, f32[16,12]{1,0:T(8,128)}, ...), branch_computations={%region_36.37_spmd, %region_37.38_spmd} | conditional | flops 31936512 | bytes 4022068 | solution.py:271
  227.5 1.9 collective-permute-start.31
  229.4 2.4 collective-permute-start.27
  231.8 2.5 collective-permute-start.29
  235.3 3.8 %collective-permute-start.33 = (f32[16,12]{0,1:T(8,128)}, f32[16,12]{0,1:T(8,128)}, u32[]{:S(2)}, u32[]{:S(2)}) collective-permute-start(f32[16,12]{0,1:T(8,128)} %log_add_fusion.1), channel_id=1, source_target_pairs={{2,0},{3,1},{4,2},{5,3},{6,4},{7,5},{8,6},{9,7},{10,8},{11,9},{12,... | collective-permute-start | bytes 2312 | tf_op jit(solution)/shard_map/ppermute | solution.py:22
  239.1 2.0 collective-permute-start.30
  241.2 1.9 collective-permute-start.32
  244.0 8.2 %collective-permute-start.35 = (f32[16,12]{1,0:T(8,128)}, f32[16,12]{1,0:T(8,128)}, u32[]{:S(2)}, u32[]{:S(2)}) collective-permute-start(f32[16,12]{1,0:T(8,128)} %get-tuple-element.471), channel_id=1, source_target_pairs={{2,0},{3,1},{4,2},{5,3},{6,4},{7,5},{8,6},{9,7},{10,8},{11,9},{12,... | collective-permute-start | bytes 2312 | tf_op jit(solution)/shard_map/ppermute | solution.py:22
  252.3 2.2 collective-permute-start.36
  254.5 6.4 %collective-permute-start.37 = (bf16[16,1536]{1,0:T(8,128)(2,1)}, bf16[16,1536]{1,0:T(8,128)(2,1)}, u32[]{:S(2)}, u32[]{:S(2)}) collective-permute-start(bf16[16,1536]{1,0:T(8,128)(2,1)} %copy_bitcast_fusion.19), channel_id=1, source_target_pairs={{1,0},{2,1},{3,2},{4,3},{5,4},{6,5},{7,6},{8,7},{9,8},{10,9},{11,1... | collective-permute-start | bytes 147464 | tf_op jit(solution)/shard_map/ppermute | solution.py:22
  261.9 2.0 collective-permute-start.38
  264.2 11.9 %collective-permute-start.39 = (bf16[16,1536]{1,0:T(8,128)(2,1)S(1)}, bf16[16,1536]{1,0:T(8,128)(2,1)S(1)}, u32[]{:S(2)}, u32[]{:S(2)}) collective-permute-start(bf16[16,1536]{1,0:T(8,128)(2,1)S(1)} %copy_bitcast_fusion.17), channel_id=1, source_target_pairs={{0,2},{1,3},{2,4},{3,5},{4,6},{5,7},{6,8},{7,9},{8,10},{9,11},{10,... | collective-permute-start | bytes 147464 | tf_op jit(solution)/shard_map/ppermute | solution.py:22
  276.1 2.7 add_add_fusion.2
  (375 shorter events, 129.4 us)
Async XLA Ops:
  0.7 64.7 %collective-permute-start.2 = (bf16[16,1536]{1,0:T(8,128)(2,1)}, bf16[16,1536]{1,0:T(8,128)(2,1)}, u32[]{:S(2)}, u32[]{:S(2)}) collective-permute-start(bf16[16,1536]{1,0:T(8,128)(2,1)} %param.35), channel_id=1, source_target_pairs={{1,0},{2,1},{3,2},{4,3},{5,4},{6,5},{7,6},{8,7},{9,8},{10,9},{11,1... | collective-permute-start | bytes 147464 | tf_op jit(solution)/shard_map/ppermute | solution.py:22
  3.5 57.7 %collective-permute-start.1 = (bf16[16,1536]{1,0:T(8,128)(2,1)}, bf16[16,1536]{1,0:T(8,128)(2,1)}, u32[]{:S(2)}, u32[]{:S(2)}) collective-permute-start(bf16[16,1536]{1,0:T(8,128)(2,1)} %param.35), channel_id=1, source_target_pairs={{0,1},{1,2},{2,3},{3,4},{4,5},{5,6},{6,7},{7,8},{8,9},{9,10},{10,1... | collective-permute-start | bytes 147464 | tf_op jit(solution)/shard_map/ppermute | solution.py:22
  5.5 51.4 %collective-permute-start = (bf16[16,1536]{1,0:T(8,128)(2,1)}, bf16[16,1536]{1,0:T(8,128)(2,1)}, u32[]{:S(2)}, u32[]{:S(2)}) collective-permute-start(bf16[16,1536]{1,0:T(8,128)(2,1)} %param.35), channel_id=1, source_target_pairs={{0,2},{1,3},{2,4},{3,5},{4,6},{5,7},{6,8},{7,9},{8,10},{9,11},{10,... | collective-permute-start | bytes 147464 | tf_op jit(solution)/shard_map/ppermute | solution.py:22
  8.6 59.5 %collective-permute-start.3 = (bf16[16,1536]{1,0:T(8,128)(2,1)}, bf16[16,1536]{1,0:T(8,128)(2,1)}, u32[]{:S(2)}, u32[]{:S(2)}) collective-permute-start(bf16[16,1536]{1,0:T(8,128)(2,1)} %param.35), channel_id=1, source_target_pairs={{2,0},{3,1},{4,2},{5,3},{6,4},{7,5},{8,6},{9,7},{10,8},{11,9},{12,... | collective-permute-start | bytes 147464 | tf_op jit(solution)/shard_map/ppermute | solution.py:22
  15.4 19.0 %collective-permute-start.4 = (bf16[16,1536]{1,0:T(8,128)(2,1)}, bf16[16,1536]{1,0:T(8,128)(2,1)}, u32[]{:S(2)}, u32[]{:S(2)}) collective-permute-start(bf16[16,1536]{1,0:T(8,128)(2,1)} %bitcast.401), channel_id=1, source_target_pairs={{0,2},{1,3},{2,4},{3,5},{4,6},{5,7},{6,8},{7,9},{8,10},{9,11},{10,... | collective-permute-start | bytes 147464 | tf_op jit(solution)/shard_map/ppermute | solution.py:22
  34.4 6.5 %collective-permute-start.5 = (bf16[16,1536]{1,0:T(8,128)(2,1)}, bf16[16,1536]{1,0:T(8,128)(2,1)S(1)}, u32[]{:S(2)}, u32[]{:S(2)}) collective-permute-start(bf16[16,1536]{1,0:T(8,128)(2,1)} %bitcast.401), channel_id=1, source_target_pairs={{0,1},{1,2},{2,3},{3,4},{4,5},{5,6},{6,7},{7,8},{8,9},{9,10},{10,1... | collective-permute-start | bytes 147464 | tf_op jit(solution)/shard_map/ppermute | solution.py:22
  40.9 4.0 %collective-permute-start.6 = (bf16[16,1536]{1,0:T(8,128)(2,1)}, bf16[16,1536]{1,0:T(8,128)(2,1)S(1)}, u32[]{:S(2)}, u32[]{:S(2)}) collective-permute-start(bf16[16,1536]{1,0:T(8,128)(2,1)} %bitcast.401), channel_id=1, source_target_pairs={{1,0},{2,1},{3,2},{4,3},{5,4},{6,5},{7,6},{8,7},{9,8},{10,9},{11,1... | collective-permute-start | bytes 147464 | tf_op jit(solution)/shard_map/ppermute | solution.py:22
  44.9 6.2 %collective-permute-start.7 = (bf16[16,1536]{1,0:T(8,128)(2,1)}, bf16[16,1536]{1,0:T(8,128)(2,1)S(1)}, u32[]{:S(2)}, u32[]{:S(2)}) collective-permute-start(bf16[16,1536]{1,0:T(8,128)(2,1)} %bitcast.401), channel_id=1, source_target_pairs={{2,0},{3,1},{4,2},{5,3},{6,4},{7,5},{8,6},{9,7},{10,8},{11,9},{12,... | collective-permute-start | bytes 147464 | tf_op jit(solution)/shard_map/ppermute | solution.py:22
  51.1 184.2 %collective-permute-start.28 = (bf16[16,1536]{1,0:T(8,128)(2,1)}, bf16[16,1536]{1,0:T(8,128)(2,1)S(1)}, u32[]{:S(2)}, u32[]{:S(2)}) collective-permute-start(bf16[16,1536]{1,0:T(8,128)(2,1)} %param.38), channel_id=1, source_target_pairs={{0,1},{1,2},{2,3},{3,4},{4,5},{5,6},{6,7},{7,8},{8,9},{9,10},{10,1... | collective-permute-start | bytes 147464 | tf_op jit(solution)/shard_map/ppermute | solution.py:22
  56.8 18.4 %collective-permute-start.14 = (bf16[16,1536]{1,0:T(8,128)(2,1)}, bf16[16,1536]{1,0:T(8,128)(2,1)}, u32[]{:S(2)}, u32[]{:S(2)}) collective-permute-start(bf16[16,1536]{1,0:T(8,128)(2,1)} %bitcast.400), channel_id=1, source_target_pairs={{2,0},{3,1},{4,2},{5,3},{6,4},{7,5},{8,6},{9,7},{10,8},{11,9},{12,... | collective-permute-start | bytes 147464 | tf_op jit(solution)/shard_map/ppermute | solution.py:22
  61.3 14.8 %collective-permute-start.12 = (bf16[16,1536]{1,0:T(8,128)(2,1)}, bf16[16,1536]{1,0:T(8,128)(2,1)}, u32[]{:S(2)}, u32[]{:S(2)}) collective-permute-start(bf16[16,1536]{1,0:T(8,128)(2,1)} %bitcast.400), channel_id=1, source_target_pairs={{1,0},{2,1},{3,2},{4,3},{5,4},{6,5},{7,6},{8,7},{9,8},{10,9},{11,1... | collective-permute-start | bytes 147464 | tf_op jit(solution)/shard_map/ppermute | solution.py:22
  65.3 12.2 %collective-permute-start.10 = (bf16[16,1536]{1,0:T(8,128)(2,1)}, bf16[16,1536]{1,0:T(8,128)(2,1)}, u32[]{:S(2)}, u32[]{:S(2)}) collective-permute-start(bf16[16,1536]{1,0:T(8,128)(2,1)} %bitcast.400), channel_id=1, source_target_pairs={{0,1},{1,2},{2,3},{3,4},{4,5},{5,6},{6,7},{7,8},{8,9},{9,10},{10,1... | collective-permute-start | bytes 147464 | tf_op jit(solution)/shard_map/ppermute | solution.py:22
  68.1 11.0 %collective-permute-start.8 = (bf16[16,1536]{1,0:T(8,128)(2,1)}, bf16[16,1536]{1,0:T(8,128)(2,1)}, u32[]{:S(2)}, u32[]{:S(2)}) collective-permute-start(bf16[16,1536]{1,0:T(8,128)(2,1)} %bitcast.400), channel_id=1, source_target_pairs={{0,2},{1,3},{2,4},{3,5},{4,6},{5,7},{6,8},{7,9},{8,10},{9,11},{10,... | collective-permute-start | bytes 147464 | tf_op jit(solution)/shard_map/ppermute | solution.py:22
  82.4 35.7 %collective-permute-start.9 = (f32[16,12]{0,1:T(8,128)}, f32[16,12]{0,1:T(8,128)}, u32[]{:S(2)}, u32[]{:S(2)}) collective-permute-start(f32[16,12]{0,1:T(8,128)} %get-tuple-element.231), channel_id=1, source_target_pairs={{2,0},{3,1},{4,2},{5,3},{6,4},{7,5},{8,6},{9,7},{10,8},{11,9},{12,... | collective-permute-start | bytes 2312 | tf_op jit(solution)/shard_map/ppermute | solution.py:22
  87.0 28.5 %collective-permute-start.16 = (f32[16,12]{0,1:T(8,128)}, f32[16,12]{0,1:T(8,128)}, u32[]{:S(2)}, u32[]{:S(2)}) collective-permute-start(f32[16,12]{0,1:T(8,128)} %get-tuple-element.236), channel_id=1, source_target_pairs={{2,0},{3,1},{4,2},{5,3},{6,4},{7,5},{8,6},{9,7},{10,8},{11,9},{12,... | collective-permute-start | bytes 2312 | tf_op jit(solution)/shard_map/ppermute | solution.py:22
  89.6 68.6 %collective-permute-start.20 = (bf16[16,1536]{1,0:T(8,128)(2,1)}, bf16[16,1536]{1,0:T(8,128)(2,1)}, u32[]{:S(2)}, u32[]{:S(2)}) collective-permute-start(bf16[16,1536]{1,0:T(8,128)(2,1)} %copy_bitcast_fusion.24), channel_id=1, source_target_pairs={{2,0},{3,1},{4,2},{5,3},{6,4},{7,5},{8,6},{9,7},{10,8},{11,9},{12,... | collective-permute-start | bytes 147464 | tf_op jit(solution)/shard_map/ppermute | solution.py:22
  95.3 35.6 %collective-permute-start.11 = (f32[16,12]{0,1:T(8,128)}, f32[16,12]{0,1:T(8,128)}, u32[]{:S(2)}, u32[]{:S(2)}) collective-permute-start(f32[16,12]{0,1:T(8,128)} %get-tuple-element.232), channel_id=1, source_target_pairs={{1,0},{2,1},{3,2},{4,3},{5,4},{6,5},{7,6},{8,7},{9,8},{10,9},{11,1... | collective-permute-start | bytes 2312 | tf_op jit(solution)/shard_map/ppermute | solution.py:22
  115.5 18.0 %collective-permute-start.17 = (f32[16,12]{0,1:T(8,128)}, f32[16,12]{0,1:T(8,128)S(1)}, u32[]{:S(2)}, u32[]{:S(2)}) collective-permute-start(f32[16,12]{0,1:T(8,128)} %get-tuple-element.237), channel_id=1, source_target_pairs={{1,0},{2,1},{3,2},{4,3},{5,4},{6,5},{7,6},{8,7},{9,8},{10,9},{11,1... | collective-permute-start | bytes 2312 | tf_op jit(solution)/shard_map/ppermute | solution.py:22
  118.1 46.4 %collective-permute-start.21 = (bf16[16,1536]{1,0:T(8,128)(2,1)}, bf16[16,1536]{1,0:T(8,128)(2,1)}, u32[]{:S(2)}, u32[]{:S(2)}) collective-permute-start(bf16[16,1536]{1,0:T(8,128)(2,1)} %copy_bitcast_fusion.23), channel_id=1, source_target_pairs={{1,0},{2,1},{3,2},{4,3},{5,4},{6,5},{7,6},{8,7},{9,8},{10,9},{11,1... | collective-permute-start | bytes 147464 | tf_op jit(solution)/shard_map/ppermute | solution.py:22
  130.9 6.1 %collective-permute-start.13 = (f32[16,12]{0,1:T(8,128)}, f32[16,12]{0,1:T(8,128)S(1)}, u32[]{:S(2)}, u32[]{:S(2)}) collective-permute-start(f32[16,12]{0,1:T(8,128)} %copy-done.71), channel_id=1, source_target_pairs={{0,1},{1,2},{2,3},{3,4},{4,5},{5,6},{6,7},{7,8},{8,9},{9,10},{10,1... | collective-permute-start | bytes 2312 | tf_op jit(solution)/shard_map/ppermute | solution.py:22
  133.5 12.7 %collective-permute-start.18 = (f32[16,12]{0,1:T(8,128)}, f32[16,12]{0,1:T(8,128)S(1)}, u32[]{:S(2)}, u32[]{:S(2)}) collective-permute-start(f32[16,12]{0,1:T(8,128)} %get-tuple-element.239), channel_id=1, source_target_pairs={{0,1},{1,2},{2,3},{3,4},{4,5},{5,6},{6,7},{7,8},{8,9},{9,10},{10,1... | collective-permute-start | bytes 2312 | tf_op jit(solution)/shard_map/ppermute | solution.py:22
  136.9 6.6 %collective-permute-start.15 = (f32[16,12]{0,1:T(8,128)}, f32[16,12]{0,1:T(8,128)S(1)}, u32[]{:S(2)}, u32[]{:S(2)}) collective-permute-start(f32[16,12]{0,1:T(8,128)} %get-tuple-element.235), channel_id=1, source_target_pairs={{0,2},{1,3},{2,4},{3,5},{4,6},{5,7},{6,8},{7,9},{8,10},{9,11},{10,... | collective-permute-start | bytes 2312 | tf_op jit(solution)/shard_map/ppermute | solution.py:22
  143.6 35.2 %collective-permute-start.22 = (bf16[16,1536]{1,0:T(8,128)(2,1)}, bf16[16,1536]{1,0:T(8,128)(2,1)}, u32[]{:S(2)}, u32[]{:S(2)}) collective-permute-start(bf16[16,1536]{1,0:T(8,128)(2,1)} %copy_bitcast_fusion.22), channel_id=1, source_target_pairs={{0,1},{1,2},{2,3},{3,4},{4,5},{5,6},{6,7},{7,8},{8,9},{9,10},{10,1... | collective-permute-start | bytes 147464 | tf_op jit(solution)/shard_map/ppermute | solution.py:22
  146.2 6.6 %collective-permute-start.19 = (f32[16,12]{0,1:T(8,128)}, f32[16,12]{0,1:T(8,128)S(1)}, u32[]{:S(2)}, u32[]{:S(2)}) collective-permute-start(f32[16,12]{0,1:T(8,128)} %get-tuple-element.240), channel_id=1, source_target_pairs={{0,2},{1,3},{2,4},{3,5},{4,6},{5,7},{6,8},{7,9},{8,10},{9,11},{10,... | collective-permute-start | bytes 2312 | tf_op jit(solution)/shard_map/ppermute | solution.py:22
  152.9 30.2 %collective-permute-start.23 = (bf16[16,1536]{1,0:T(8,128)(2,1)}, bf16[16,1536]{1,0:T(8,128)(2,1)}, u32[]{:S(2)}, u32[]{:S(2)}) collective-permute-start(bf16[16,1536]{1,0:T(8,128)(2,1)} %copy_bitcast_fusion.21), channel_id=1, source_target_pairs={{0,2},{1,3},{2,4},{3,5},{4,6},{5,7},{6,8},{7,9},{8,10},{9,11},{10,... | collective-permute-start | bytes 147464 | tf_op jit(solution)/shard_map/ppermute | solution.py:22
  158.2 9.1 %collective-permute-start.40 = (bf16[16,1536]{1,0:T(8,128)(2,1)}, bf16[16,1536]{1,0:T(8,128)(2,1)}, u32[]{:S(2)}, u32[]{:S(2)}) collective-permute-start(bf16[16,1536]{1,0:T(8,128)(2,1)} %bitcast.441), channel_id=1, source_target_pairs={{2,0},{3,1},{4,2},{5,3},{6,4},{7,5},{8,6},{9,7},{10,8},{11,9},{12,... | collective-permute-start | bytes 147464 | tf_op jit(solution)/shard_map/ppermute | solution.py:22
  164.5 36.3 %collective-permute-start.44 = (bf16[16,1536]{1,0:T(8,128)(2,1)}, bf16[16,1536]{1,0:T(8,128)(2,1)}, u32[]{:S(2)}, u32[]{:S(2)}) collective-permute-start(bf16[16,1536]{1,0:T(8,128)(2,1)} %bitcast.437), channel_id=1, source_target_pairs={{2,0},{3,1},{4,2},{5,3},{6,4},{7,5},{8,6},{9,7},{10,8},{11,9},{12,... | collective-permute-start | bytes 147464 | tf_op jit(solution)/shard_map/ppermute | solution.py:22
  167.3 5.0 %collective-permute-start.41 = (bf16[16,1536]{1,0:T(8,128)(2,1)}, bf16[16,1536]{1,0:T(8,128)(2,1)S(1)}, u32[]{:S(2)}, u32[]{:S(2)}) collective-permute-start(bf16[16,1536]{1,0:T(8,128)(2,1)} %bitcast.440), channel_id=1, source_target_pairs={{1,0},{2,1},{3,2},{4,3},{5,4},{6,5},{7,6},{8,7},{9,8},{10,9},{11,1... | collective-permute-start | bytes 147464 | tf_op jit(solution)/shard_map/ppermute | solution.py:22
  172.3 31.2 %collective-permute-start.46 = (bf16[16,1536]{1,0:T(8,128)(2,1)}, bf16[16,1536]{1,0:T(8,128)(2,1)}, u32[]{:S(2)}, u32[]{:S(2)}) collective-permute-start(bf16[16,1536]{1,0:T(8,128)(2,1)} %bitcast.436), channel_id=1, source_target_pairs={{0,1},{1,2},{2,3},{3,4},{4,5},{5,6},{6,7},{7,8},{8,9},{9,10},{10,1... | collective-permute-start | bytes 147464 | tf_op jit(solution)/shard_map/ppermute | solution.py:22
  178.8 28.8 %collective-permute-start.47 = (bf16[16,1536]{1,0:T(8,128)(2,1)}, bf16[16,1536]{1,0:T(8,128)(2,1)}, u32[]{:S(2)}, u32[]{:S(2)}) collective-permute-start(bf16[16,1536]{1,0:T(8,128)(2,1)} %bitcast.435), channel_id=1, source_target_pairs={{0,2},{1,3},{2,4},{3,5},{4,6},{5,7},{6,8},{7,9},{8,10},{9,11},{10,... | collective-permute-start | bytes 147464 | tf_op jit(solution)/shard_map/ppermute | solution.py:22
  183.1 6.6 %collective-permute-start.42 = (bf16[16,1536]{1,0:T(8,128)(2,1)}, bf16[16,1536]{1,0:T(8,128)(2,1)}, u32[]{:S(2)}, u32[]{:S(2)}) collective-permute-start(bf16[16,1536]{1,0:T(8,128)(2,1)} %bitcast.439), channel_id=1, source_target_pairs={{0,1},{1,2},{2,3},{3,4},{4,5},{5,6},{6,7},{7,8},{8,9},{9,10},{10,1... | collective-permute-start | bytes 147464 | tf_op jit(solution)/shard_map/ppermute | solution.py:22
  189.7 7.1 %collective-permute-start.43 = (bf16[16,1536]{1,0:T(8,128)(2,1)}, bf16[16,1536]{1,0:T(8,128)(2,1)S(1)}, u32[]{:S(2)}, u32[]{:S(2)}) collective-permute-start(bf16[16,1536]{1,0:T(8,128)(2,1)} %bitcast.438), channel_id=1, source_target_pairs={{0,2},{1,3},{2,4},{3,5},{4,6},{5,7},{6,8},{7,9},{8,10},{9,11},{10,... | collective-permute-start | bytes 147464 | tf_op jit(solution)/shard_map/ppermute | solution.py:22
  196.8 12.8 %collective-permute-start.45 = (bf16[16,1536]{1,0:T(8,128)(2,1)}, bf16[16,1536]{1,0:T(8,128)(2,1)S(1)}, u32[]{:S(2)}, u32[]{:S(2)}) collective-permute-start(bf16[16,1536]{1,0:T(8,128)(2,1)} %bitcast.434), channel_id=1, source_target_pairs={{1,0},{2,1},{3,2},{4,3},{5,4},{6,5},{7,6},{8,7},{9,8},{10,9},{11,1... | collective-permute-start | bytes 147464 | tf_op jit(solution)/shard_map/ppermute | solution.py:22
  200.8 26.6 %collective-permute-start.25 = (bf16[16,1536]{1,0:T(8,128)(2,1)}, bf16[16,1536]{1,0:T(8,128)(2,1)}, u32[]{:S(2)}, u32[]{:S(2)}) collective-permute-start(bf16[16,1536]{1,0:T(8,128)(2,1)} %param.38), channel_id=1, source_target_pairs={{0,2},{1,3},{2,4},{3,5},{4,6},{5,7},{6,8},{7,9},{8,10},{9,11},{10,... | collective-permute-start | bytes 147464 | tf_op jit(solution)/shard_map/ppermute | solution.py:22
  203.5 58.4 %collective-permute-start.34 = (bf16[16,1536]{1,0:T(8,128)(2,1)}, bf16[16,1536]{1,0:T(8,128)(2,1)}, u32[]{:S(2)}, u32[]{:S(2)}) collective-permute-start(bf16[16,1536]{1,0:T(8,128)(2,1)} %param.38), channel_id=1, source_target_pairs={{2,0},{3,1},{4,2},{5,3},{6,4},{7,5},{8,6},{9,7},{10,8},{11,9},{12,... | collective-permute-start | bytes 147464 | tf_op jit(solution)/shard_map/ppermute | solution.py:22
  207.6 21.8 %collective-permute-start.24 = (f32[16,12]{0,1:T(8,128)}, f32[16,12]{0,1:T(8,128)}, u32[]{:S(2)}, u32[]{:S(2)}) collective-permute-start(f32[16,12]{0,1:T(8,128)} %log_add_fusion.1), channel_id=1, source_target_pairs={{0,2},{1,3},{2,4},{3,5},{4,6},{5,7},{6,8},{7,9},{8,10},{9,11},{10,... | collective-permute-start | bytes 2312 | tf_op jit(solution)/shard_map/ppermute | solution.py:22
  209.6 22.2 %collective-permute-start.26 = (f32[16,12]{1,0:T(8,128)}, f32[16,12]{1,0:T(8,128)}, u32[]{:S(2)}, u32[]{:S(2)}) collective-permute-start(f32[16,12]{1,0:T(8,128)} %get-tuple-element.471), channel_id=1, source_target_pairs={{0,2},{1,3},{2,4},{3,5},{4,6},{5,7},{6,8},{7,9},{8,10},{9,11},{10,... | collective-permute-start | bytes 2312 | tf_op jit(solution)/shard_map/ppermute | solution.py:22
  227.5 16.6 %collective-permute-start.31 = (bf16[16,1536]{1,0:T(8,128)(2,1)}, bf16[16,1536]{1,0:T(8,128)(2,1)}, u32[]{:S(2)}, u32[]{:S(2)}) collective-permute-start(bf16[16,1536]{1,0:T(8,128)(2,1)} %param.38), channel_id=1, source_target_pairs={{1,0},{2,1},{3,2},{4,3},{5,4},{6,5},{7,6},{8,7},{9,8},{10,9},{11,1... | collective-permute-start | bytes 147464 | tf_op jit(solution)/shard_map/ppermute | solution.py:22
  229.4 9.7 %collective-permute-start.27 = (f32[16,12]{0,1:T(8,128)}, f32[16,12]{0,1:T(8,128)}, u32[]{:S(2)}, u32[]{:S(2)}) collective-permute-start(f32[16,12]{0,1:T(8,128)} %log_add_fusion.1), channel_id=1, source_target_pairs={{0,1},{1,2},{2,3},{3,4},{4,5},{5,6},{6,7},{7,8},{8,9},{9,10},{10,1... | collective-permute-start | bytes 2312 | tf_op jit(solution)/shard_map/ppermute | solution.py:22
  231.8 9.3 %collective-permute-start.29 = (f32[16,12]{1,0:T(8,128)}, f32[16,12]{1,0:T(8,128)}, u32[]{:S(2)}, u32[]{:S(2)}) collective-permute-start(f32[16,12]{1,0:T(8,128)} %get-tuple-element.471), channel_id=1, source_target_pairs={{0,1},{1,2},{2,3},{3,4},{4,5},{5,6},{6,7},{7,8},{8,9},{9,10},{10,1... | collective-permute-start | bytes 2312 | tf_op jit(solution)/shard_map/ppermute | solution.py:22
  235.3 28.6 %collective-permute-start.33 = (f32[16,12]{0,1:T(8,128)}, f32[16,12]{0,1:T(8,128)}, u32[]{:S(2)}, u32[]{:S(2)}) collective-permute-start(f32[16,12]{0,1:T(8,128)} %log_add_fusion.1), channel_id=1, source_target_pairs={{2,0},{3,1},{4,2},{5,3},{6,4},{7,5},{8,6},{9,7},{10,8},{11,9},{12,... | collective-permute-start | bytes 2312 | tf_op jit(solution)/shard_map/ppermute | solution.py:22
  239.1 13.1 %collective-permute-start.30 = (f32[16,12]{0,1:T(8,128)}, f32[16,12]{0,1:T(8,128)}, u32[]{:S(2)}, u32[]{:S(2)}) collective-permute-start(f32[16,12]{0,1:T(8,128)} %log_add_fusion.1), channel_id=1, source_target_pairs={{1,0},{2,1},{3,2},{4,3},{5,4},{6,5},{7,6},{8,7},{9,8},{10,9},{11,1... | collective-permute-start | bytes 2312 | tf_op jit(solution)/shard_map/ppermute | solution.py:22
  241.2 13.3 %collective-permute-start.32 = (f32[16,12]{1,0:T(8,128)}, f32[16,12]{1,0:T(8,128)}, u32[]{:S(2)}, u32[]{:S(2)}) collective-permute-start(f32[16,12]{1,0:T(8,128)} %get-tuple-element.471), channel_id=1, source_target_pairs={{1,0},{2,1},{3,2},{4,3},{5,4},{6,5},{7,6},{8,7},{9,8},{10,9},{11,1... | collective-permute-start | bytes 2312 | tf_op jit(solution)/shard_map/ppermute | solution.py:22
  244.0 19.9 %collective-permute-start.35 = (f32[16,12]{1,0:T(8,128)}, f32[16,12]{1,0:T(8,128)}, u32[]{:S(2)}, u32[]{:S(2)}) collective-permute-start(f32[16,12]{1,0:T(8,128)} %get-tuple-element.471), channel_id=1, source_target_pairs={{2,0},{3,1},{4,2},{5,3},{6,4},{7,5},{8,6},{9,7},{10,8},{11,9},{12,... | collective-permute-start | bytes 2312 | tf_op jit(solution)/shard_map/ppermute | solution.py:22
  252.3 34.3 %collective-permute-start.36 = (bf16[16,1536]{1,0:T(8,128)(2,1)}, bf16[16,1536]{1,0:T(8,128)(2,1)}, u32[]{:S(2)}, u32[]{:S(2)}) collective-permute-start(bf16[16,1536]{1,0:T(8,128)(2,1)} %copy_bitcast_fusion.20), channel_id=1, source_target_pairs={{2,0},{3,1},{4,2},{5,3},{6,4},{7,5},{8,6},{9,7},{10,8},{11,9},{12,... | collective-permute-start | bytes 147464 | tf_op jit(solution)/shard_map/ppermute | solution.py:22
  254.5 32.9 %collective-permute-start.37 = (bf16[16,1536]{1,0:T(8,128)(2,1)}, bf16[16,1536]{1,0:T(8,128)(2,1)}, u32[]{:S(2)}, u32[]{:S(2)}) collective-permute-start(bf16[16,1536]{1,0:T(8,128)(2,1)} %copy_bitcast_fusion.19), channel_id=1, source_target_pairs={{1,0},{2,1},{3,2},{4,3},{5,4},{6,5},{7,6},{8,7},{9,8},{10,9},{11,1... | collective-permute-start | bytes 147464 | tf_op jit(solution)/shard_map/ppermute | solution.py:22
  261.9 26.3 %collective-permute-start.38 = (bf16[16,1536]{1,0:T(8,128)(2,1)}, bf16[16,1536]{1,0:T(8,128)(2,1)}, u32[]{:S(2)}, u32[]{:S(2)}) collective-permute-start(bf16[16,1536]{1,0:T(8,128)(2,1)} %copy_bitcast_fusion.18), channel_id=1, source_target_pairs={{0,1},{1,2},{2,3},{3,4},{4,5},{5,6},{6,7},{7,8},{8,9},{9,10},{10,1... | collective-permute-start | bytes 147464 | tf_op jit(solution)/shard_map/ppermute | solution.py:22
  264.2 24.8 %collective-permute-start.39 = (bf16[16,1536]{1,0:T(8,128)(2,1)S(1)}, bf16[16,1536]{1,0:T(8,128)(2,1)S(1)}, u32[]{:S(2)}, u32[]{:S(2)}) collective-permute-start(bf16[16,1536]{1,0:T(8,128)(2,1)S(1)} %copy_bitcast_fusion.17), channel_id=1, source_target_pairs={{0,2},{1,3},{2,4},{3,5},{4,6},{5,7},{6,8},{7,9},{8,10},{9,11},{10,... | collective-permute-start | bytes 147464 | tf_op jit(solution)/shard_map/ppermute | solution.py:22
  (69 other events, 635.8 us)
where the time goes:
time: 295 us; the launch traced here: 291 us
  starting transfers between devices  159 us (54%)
  local copies, waits for them, and re-layouts  70.1 us (24%)
  other arithmetic  23.2 us (8%)
  waiting for transfers between devices  20 us (7%)
  matrix products  12.8 us (4%)
  between operations  5.77 us (2%)
    ppermute x48, starting transfers between devices, passed_along(): return lax.ppermute(block, axis, route)  159 us
    unnamed x171, local copies, waits for them, and re-layouts  26.8 us
    ppermute x48, waiting for transfers between devices, passed_along(): return lax.ppermute(block, axis, route)  20 us
    another operation x29, local copies, waits for them, and re-layouts  9.65 us
  transfers between devices with their start and end apart: 48, of which 8 were waited for; matrix products, arithmetic and copies ran while one was open for 34% of the time, Pallas kernels for 0%

commit v1 on v0

v1 whole, which is shorter than its diff:
```python
import functools
import math

import jax
import jax.numpy as jnp
from jax import lax
from jax.experimental import pallas as pl
from jax.experimental.pallas import tpu as pltpu
from jax.sharding import PartitionSpec as P

DH = 128
FRAME = 960
AFRAME = 96
R = 2
SPAN = 5
EPSILON = 1e-06
HUGE = 1e30
SCALE = DH ** (-0.5)
SLOTS = (0, 1, 3, 4)
REACH = 2 * R
AUDIO_Q, AUDIO_DOUT, AUDIO_K, AUDIO_V = range(4)
D_KEY, D_VALUE, D_QUERY = range(3)
f32 = jnp.float32
bf16 = jnp.bfloat16


def nt(a, b):
    return lax.dot_general(a, b, (((1,), (1,)), ((), ())), preferred_element_type=f32)


def nn(a, b):
    return lax.dot_general(a, b, (((1,), (0,)), ((), ())), preferred_element_type=f32)


def tn(a, b):
    return lax.dot_general(a, b, (((0,), (0,)), ((), ())), preferred_element_type=f32)


def swapped(x):
    return pltpu.roll(x, DH // 2, 1)


def rinv_of(x):
    return lax.rsqrt(jnp.mean(x * x, axis=-1, keepdims=True) + EPSILON)


def turn(x, rinv, gain, cosine, sine):
    n = x * rinv * gain
    return n * cosine + swapped(n) * sine


def turn_back(dy, x, rinv, gain, cosine, sine):
    dn = dy * cosine - swapped(dy) * sine
    hat = x * rinv
    dh = dn * gain
    return rinv * (dh - hat * jnp.mean(dh * hat, axis=-1, keepdims=True))


def tables(places):
    lane = lax.broadcasted_iota(jnp.int32, places.shape, 1)
    half = DH // 2
    channel = jnp.where(lane < half, lane, lane - half).astype(f32)
    angles = places * jnp.exp(channel * (-2.0 * math.log(10000.0) / DH))
    sine = jnp.sin(angles)
    return jnp.cos(angles), jnp.where(lane < half, -sine, sine)


def kernel(
    along, count, vq, vk, vv, aq, ak, av, gain, vdo, ado, link,
    o_v, o_a, g_vq, g_vk, g_vv, g_aq, g_ak, g_av,
    win, po, po_in, gr, gr_in, stat, qv, kv, ea, dpa, pab, gab, rq, rk, tab_v, tab_a, coef, bias, wts,
    s_win, r_win, s_stat, r_stat, s_po, r_po, s_gr, r_gr,
):
    vrows, hd = vq.shape
    arows = aq.shape[0]
    heads = hd // DH
    wrows = SPAN * arows
    clip = lax.axis_index("clips")
    me = lax.axis_index("video") * along + lax.axis_index("audio")

    def valid(i):
        return jnp.logical_and(i >= 0, i < count)

    def device(i):
        return (clip, i // along, lax.rem(i, along))

    def rows(j):
        return pl.ds(j * arows, arows)

    def lanes(h):
        return pl.ds(pl.multiple_of(h * DH, DH), DH)

    others = [d for d in range(-REACH, REACH + 1) if d]

    barrier = pltpu.get_barrier_semaphore()
    for d in others:

        @pl.when(valid(me + d))
        def _():
            pl.semaphore_signal(
                barrier, inc=1, device_id=device(me + d), device_id_type=pl.DeviceIdType.MESH
            )

    row = lax.broadcasted_iota(jnp.int32, (arows, DH), 0)
    c, s = tables((me * arows + row).astype(f32) / AFRAME)
    tab_a[0], tab_a[1] = c, s
    vplace = jnp.zeros((8, DH), jnp.int32) + (me * vrows) // FRAME
    c, s = tables(vplace.astype(f32))
    tab_v[0], tab_v[1] = c, s

    def audio_prepare(h, _):
        hs = lanes(h)
        for src, slot, g in ((aq, AUDIO_Q, 2), (ak, AUDIO_K, 3)):
            x = src[:, hs].astype(f32)
            y = turn(x, rinv_of(x), gain[g : g + 1, hs], tab_a[0], tab_a[1])
            win[slot, rows(R), hs] = y.astype(bf16)
        return 0

    lax.fori_loop(0, heads, audio_prepare, 0)
    win[AUDIO_DOUT, rows(R), :] = ado[...]
    win[AUDIO_V, rows(R), :] = av[...]

    pl.semaphore_wait(barrier, jnp.minimum(me, REACH) + jnp.minimum(count - 1 - me, REACH))

    def win_copy(member, n, to):
        j = SLOTS[n]
        return pltpu.make_async_remote_copy(
            src_ref=win.at[member, rows(R)],
            dst_ref=win.at[member, rows(j)],
            send_sem=s_win.at[member, n],
            recv_sem=r_win.at[member, n],
            device_id=device(to),
            device_id_type=pl.DeviceIdType.MESH,
        )

    def back_copy(src, dst, send, recv, n, to):
        j = SLOTS[n]
        return pltpu.make_async_remote_copy(
            src_ref=src.at[rows(j)],
            dst_ref=dst.at[rows(j)],
            send_sem=send.at[n],
            recv_sem=recv.at[n],
            device_id=device(to),
            device_id_type=pl.DeviceIdType.MESH,
        )

    def stat_copy(d, to):
        n = others.index(d)
        return pltpu.make_async_remote_copy(
            src_ref=stat.at[REACH],
            dst_ref=stat.at[REACH - d],
            send_sem=s_stat.at[n],
            recv_sem=r_stat.at[n],
            device_id=device(to),
            device_id_type=pl.DeviceIdType.MESH,
        )

    def win_each(members, action):
        for member in members:
            for n, j in enumerate(SLOTS):
                other = me + j - R if action == "wait_recv" else me + R - j

                @pl.when(valid(other))
                def _():
                    getattr(win_copy(member, n, other), action)()

    def back_each(src, dst, send, recv, action):
        for n, j in enumerate(SLOTS):
            other = me + R - j if action == "wait_recv" else me + j - R

            @pl.when(valid(other))
            def _():
                getattr(back_copy(src, dst, send, recv, n, other), action)()

    def stat_each(action):
        for d in others:
            other = me - d if action == "wait_recv" else me + d

            @pl.when(valid(other))
            def _():
                getattr(stat_copy(d, other), action)()

    win_each((AUDIO_Q, AUDIO_DOUT, AUDIO_K, AUDIO_V), "start")

    for j in SLOTS:

        @pl.when(jnp.logical_not(valid(me + j - R)))
        def _():
            for member in range(4):
                win[member, rows(j), :] = jnp.zeros((arows, hd), bf16)

        @pl.when(jnp.logical_not(valid(me + R - j)))
        def _():
            po_in[rows(j), :] = jnp.zeros((arows, hd), bf16)
            for member in range(3):
                gr_in[member, rows(j), :] = jnp.zeros((arows, hd), bf16)

    empty = jnp.where(lax.broadcasted_iota(jnp.int32, (48, DH), 0) < 16, -HUGE, 0.0)
    stat[REACH] = empty
    for d in others:

        @pl.when(jnp.logical_not(valid(me - d)))
        def _():
            stat[REACH - d] = empty

    lane_slot = lax.broadcasted_iota(jnp.int32, (1, wrows), 1) // arows
    linked_row = jnp.zeros((1, wrows), jnp.int32)
    for j in range(SPAN):
        on = link[0, j]
        bias[rows(j), :] = jnp.zeros((arows, vrows), f32) + jnp.where(on > 0, 0.0, -HUGE)
        linked_row = jnp.where(lane_slot == j, on, linked_row)
    linked_row = linked_row > 0

    def video_prepare(h, _):
        hs = lanes(h)
        for src, dst, keep, g in ((vq, qv, rq, 0), (vk, kv, rk, 1)):
            x = src[:, hs].astype(f32)
            rinv = rinv_of(x)
            keep[:, hs] = jnp.broadcast_to(rinv, (vrows, DH))
            y = turn(x, rinv, gain[g : g + 1, hs], tab_v[0, 0:1], tab_v[1, 0:1])
            dst[:, hs] = y.astype(bf16)
        return 0

    lax.fori_loop(0, heads, video_prepare, 0)

    win_each((AUDIO_Q, AUDIO_DOUT), "wait_recv")

    def audio_forward(h, _):
        hs = lanes(h)
        v = vv[:, hs]
        r = nt(kv[:, hs], win[AUDIO_Q, :, hs]) * SCALE
        top = jnp.max(r, axis=0, keepdims=True)
        e = jnp.exp(r - top)
        ea[h] = e
        dp = nt(v, win[AUDIO_DOUT, :, hs])
        dpa[h] = dp
        stat[REACH, pl.ds(h, 1), 0:wrows] = jnp.where(linked_row, top, -HUGE)
        stat[REACH, pl.ds(16 + h, 1), 0:wrows] = jnp.where(
            linked_row, jnp.sum(e, axis=0, keepdims=True), 0.0
        )
        stat[REACH, pl.ds(32 + h, 1), 0:wrows] = jnp.where(
            linked_row, jnp.sum(e * dp, axis=0, keepdims=True), 0.0
        )
        po[:, hs] = tn(e.astype(bf16), v).astype(bf16)
        return 0

    lax.fori_loop(0, heads, audio_forward, 0)
    stat_each("start")
    back_each(po, po_in, s_po, r_po, "start")

    win_each((AUDIO_K, AUDIO_V), "wait_recv")

    def video_side(h, _):
        hs = lanes(h)
        ka, va = win[AUDIO_K, :, hs], win[AUDIO_V, :, hs]
        q, do = qv[:, hs], vdo[:, hs]
        sc = nt(ka, q) * SCALE + bias[...]
        top = jnp.max(sc, axis=0, keepdims=True)
        e = jnp.exp(sc - top)
        p = e * (1.0 / jnp.sum(e, axis=0, keepdims=True))
        pb = p.astype(bf16)
        o_v[:, hs] = tn(pb, va).astype(bf16)
        dp = nt(va, do)
        delta = jnp.sum(p * dp, axis=0, keepdims=True)
        gs = (p * (dp - delta)).astype(bf16)
        gr[D_KEY, :, hs] = (nn(gs, q) * SCALE).astype(bf16)
        gr[D_VALUE, :, hs] = nn(pb, do).astype(bf16)
        dq = tn(gs, ka) * SCALE
        g_vq[:, hs] = turn_back(
            dq, vq[:, hs].astype(f32), rq[:, hs], gain[0:1, hs], tab_v[0, 0:1], tab_v[1, 0:1]
        ).astype(bf16)
        return 0

    lax.fori_loop(0, heads, video_side, 0)
    for member in (D_KEY, D_VALUE):
        back_each(gr.at[member], gr_in.at[member], s_gr.at[member], r_gr.at[member], "start")

    stat_each("wait_recv")
    lane = lax.broadcasted_iota(jnp.int32, (16, DH), 1)
    tops, totals, dots = [], [], []
    for t in range(2 * REACH + 1):
        shift = (t - REACH) * arows
        inside = jnp.logical_and(lane >= shift, lane < shift + wrows)
        rolled = [
            pltpu.roll(stat[t, 16 * i : 16 * i + 16], shift % DH, 1) if shift else stat[t, 16 * i : 16 * i + 16]
            for i in range(3)
        ]
        tops.append(jnp.where(inside, rolled[0], -HUGE))
        totals.append(jnp.where(inside, rolled[1], 0.0))
        dots.append(jnp.where(inside, rolled[2], 0.0))
    best = functools.reduce(jnp.maximum, tops)
    factors = [jnp.where(a > -0.5 * HUGE, jnp.exp(a - best), 0.0) for a in tops]
    total = sum(a * b for a, b in zip(factors, totals))
    inverse = 1.0 / jnp.where(total > 0.0, total, 1.0)
    coef[0] = factors[REACH] * inverse
    coef[1] = sum(a * b for a, b in zip(factors, dots)) * inverse
    wts[...] = jnp.zeros(wts.shape, f32)
    for j in range(SPAN):
        wts[16 * j : 16 * j + 16, :] = factors[REACH + R - j] * inverse

    def audio_back(h, _):
        hs = lanes(h)
        p = ea[h] * coef[0, pl.ds(h, 1), 0:wrows]
        ga = (p * (dpa[h] - coef[1, pl.ds(h, 1), 0:wrows])).astype(bf16)
        pab[h] = p.astype(bf16)
        gab[h] = ga
        gr[D_QUERY, :, hs] = (tn(ga, kv[:, hs]) * SCALE).astype(bf16)
        return 0

    lax.fori_loop(0, heads, audio_back, 0)
    back_each(gr.at[D_QUERY], gr_in.at[D_QUERY], s_gr.at[D_QUERY], r_gr.at[D_QUERY], "start")

    def video_back(h, _):
        hs = lanes(h)
        g_vv[:, hs] = nn(pab[h], win[AUDIO_DOUT, :, hs]).astype(bf16)
        dk = nn(gab[h], win[AUDIO_Q, :, hs]) * SCALE
        g_vk[:, hs] = turn_back(
            dk, vk[:, hs].astype(f32), rk[:, hs], gain[1:2, hs], tab_v[0, 0:1], tab_v[1, 0:1]
        ).astype(bf16)
        return 0

    lax.fori_loop(0, heads, video_back, 0)

    turned = jnp.transpose(wts[...])[R * arows : (R + 1) * arows, :]
    back_each(po, po_in, s_po, r_po, "wait_recv")
    for h in range(heads):
        hs = slice(h * DH, (h + 1) * DH)
        acc = jnp.zeros((arows, DH), f32)
        for j in range(SPAN):
            part = (po if j == R else po_in)[j * arows : (j + 1) * arows, hs].astype(f32)
            acc += turned[:, 16 * j + h : 16 * j + h + 1] * part
        o_a[:, hs] = acc.astype(bf16)

    def merged(member, hs):
        acc = gr[member, rows(R), hs].astype(f32)
        for j in SLOTS:
            acc += gr_in[member, rows(j), hs].astype(f32)
        return acc

    def audio_grad(src, member, g, dst):
        def body(h, _):
            hs = lanes(h)
            x = src[:, hs].astype(f32)
            dst[:, hs] = turn_back(
                merged(member, hs), x, rinv_of(x), gain[g : g + 1, hs], tab_a[0], tab_a[1]
            ).astype(bf16)
            return 0

        lax.fori_loop(0, heads, body, 0)

    for member in (D_KEY, D_VALUE):
        back_each(gr.at[member], gr_in.at[member], s_gr.at[member], r_gr.at[member], "wait_recv")
    g_av[...] = merged(D_VALUE, slice(None)).astype(bf16)
    audio_grad(ak, D_KEY, 3, g_ak)
    back_each(gr.at[D_QUERY], gr_in.at[D_QUERY], s_gr.at[D_QUERY], r_gr.at[D_QUERY], "wait_recv")
    audio_grad(aq, D_QUERY, 2, g_aq)

    win_each(range(4), "wait_send")
    stat_each("wait_send")
    back_each(po, po_in, s_po, r_po, "wait_send")
    for member in range(3):
        back_each(gr.at[member], gr_in.at[member], s_gr.at[member], r_gr.at[member], "wait_send")


def on_device(along, count, *args):
    vq, aq = args[0], args[3]
    vrows, hd = vq.shape
    arows = aq.shape[0]
    heads = hd // DH
    wrows = SPAN * arows
    video = jax.ShapeDtypeStruct((vrows, hd), bf16)
    audio = jax.ShapeDtypeStruct((arows, hd), bf16)
    vmem = pl.BlockSpec(memory_space=pltpu.VMEM)
    dma = pltpu.SemaphoreType.DMA
    n = len(SLOTS)
    scratch = [
        pltpu.VMEM((4, wrows, hd), bf16),
        pltpu.VMEM((wrows, hd), bf16),
        pltpu.VMEM((wrows, hd), bf16),
        pltpu.VMEM((3, wrows, hd), bf16),
        pltpu.VMEM((3, wrows, hd), bf16),
        pltpu.VMEM((2 * REACH + 1, 48, DH), f32),
        pltpu.VMEM((vrows, hd), bf16),
        pltpu.VMEM((vrows, hd), bf16),
        pltpu.VMEM((heads, vrows, wrows), f32),
        pltpu.VMEM((heads, vrows, wrows), f32),
        pltpu.VMEM((heads, vrows, wrows), bf16),
        pltpu.VMEM((heads, vrows, wrows), bf16),
        pltpu.VMEM((vrows, hd), f32),
        pltpu.VMEM((vrows, hd), f32),
        pltpu.VMEM((2, 8, DH), f32),
        pltpu.VMEM((2, arows, DH), f32),
        pltpu.VMEM((2, 16, DH), f32),
        pltpu.VMEM((wrows, vrows), f32),
        pltpu.VMEM((DH, DH), f32),
        dma((4, n)), dma((4, n)),
        dma((2 * REACH,)), dma((2 * REACH,)),
        dma((n,)), dma((n,)),
        dma((3, n)), dma((3, n)),
    ]
    return pl.pallas_call(
        functools.partial(kernel, along, count),
        out_shape=[video, audio, video, video, video, audio, audio, audio],
        in_specs=[vmem] * 9 + [pl.BlockSpec(memory_space=pltpu.SMEM)],
        out_specs=[vmem] * 8,
        scratch_shapes=scratch,
        compiler_params=pltpu.CompilerParams(
            collective_id=0, has_side_effects=True, vmem_limit_bytes=40 * 1024 * 1024
        ),
        name="linked_attention",
    )(*args)


def solution(mesh):
    along = mesh.shape["audio"]
    count = mesh.shape["video"] * along
    rows = P(("clips", "video", "audio"), None)
    return jax.shard_map(
        functools.partial(on_device, along, count),
        mesh=mesh,
        in_specs=(rows,) * 6 + (P(),) + (rows,) * 3,
        out_specs=(rows,) * 8,
        check_vma=False,
    )
```

time: 295 us -> 59.1 us (0.20)
  the two profiles are of different devices: /device:TPU:20 before, /device:TPU:15 now
where the time goes in v1:
time: 59.1 us; the launch traced here: 58.5 us
  Pallas kernels  43.6 us (74%)
  local copies, waits for them, and re-layouts  14.3 us (24%)
  between operations  0.67 us (1%)
    pallas_call x1, Pallas kernels, on_device(): pl.pallas_call(functools.partial(kernel, along, count), out_shape=[video,...  43.6 us
    unnamed x28, local copies, waits for them, and re-layouts  14.3 us

profile of v1, /device:TPU:15, one launch (start us, length us, event | category | flops | bytes accessed | tf_op | source)
XLA Modules:
  0.0 58.5 jit_solution(3600147559492784150)
XLA Ops:
  0.6 0.0 copy-start
  0.6 1.0 %copy-done = bf16[160,1536]{1,0:T(8,128)(2,1)S(1)} copy-done((bf16[160,1536]{1,0:T(8,128)(2,1)S(1)}, bf16[160,1536]{1,0:T(8,128)(2,1)}, u32[]{:S(2)}) %copy-start) | copy-done | bytes 491544
  1.7 0.0 copy-start.1
  1.7 1.0 %copy-done.1 = bf16[160,1536]{1,0:T(8,128)(2,1)S(1)} copy-done((bf16[160,1536]{1,0:T(8,128)(2,1)S(1)}, bf16[160,1536]{1,0:T(8,128)(2,1)}, u32[]{:S(2)}) %copy-start.1) | copy-done | bytes 491544
  2.7 0.0 copy-start.2
  2.7 1.0 %copy-done.2 = bf16[160,1536]{1,0:T(8,128)(2,1)S(1)} copy-done((bf16[160,1536]{1,0:T(8,128)(2,1)S(1)}, bf16[160,1536]{1,0:T(8,128)(2,1)}, u32[]{:S(2)}) %copy-start.2) | copy-done | bytes 491544
  3.7 0.0 copy-start.3
  3.7 1.0 %copy-done.3 = bf16[160,1536]{1,0:T(8,128)(2,1)S(1)} copy-done((bf16[160,1536]{1,0:T(8,128)(2,1)S(1)}, bf16[160,1536]{1,0:T(8,128)(2,1)}, u32[]{:S(2)}) %copy-start.3) | copy-done | bytes 491544
  4.8 0.0 copy-start.4
  4.8 0.8 %copy-done.4 = bf16[16,1536]{1,0:T(8,128)(2,1)S(1)} copy-done((bf16[16,1536]{1,0:T(8,128)(2,1)S(1)}, bf16[16,1536]{1,0:T(8,128)(2,1)}, u32[]{:S(2)}) %copy-start.4) | copy-done | bytes 49176
  5.6 0.0 copy-start.5
  5.6 0.8 %copy-done.5 = bf16[16,1536]{1,0:T(8,128)(2,1)S(1)} copy-done((bf16[16,1536]{1,0:T(8,128)(2,1)S(1)}, bf16[16,1536]{1,0:T(8,128)(2,1)}, u32[]{:S(2)}) %copy-start.5) | copy-done | bytes 49176
  6.4 0.0 copy-start.6
  6.4 0.8 %copy-done.6 = bf16[16,1536]{1,0:T(8,128)(2,1)S(1)} copy-done((bf16[16,1536]{1,0:T(8,128)(2,1)S(1)}, bf16[16,1536]{1,0:T(8,128)(2,1)}, u32[]{:S(2)}) %copy-start.6) | copy-done | bytes 49176
  7.2 0.0 copy-start.7
  7.2 0.8 %copy-done.7 = bf16[16,1536]{1,0:T(8,128)(2,1)S(1)} copy-done((bf16[16,1536]{1,0:T(8,128)(2,1)S(1)}, bf16[16,1536]{1,0:T(8,128)(2,1)}, u32[]{:S(2)}) %copy-start.7) | copy-done | bytes 49176
  8.0 0.0 copy-start.8
  8.0 0.7 %copy-done.8 = f32[4,1536]{1,0:T(4,128)S(1)} copy-done((f32[4,1536]{1,0:T(4,128)S(1)}, f32[4,1536]{1,0:T(4,128)}, u32[]{:S(2)}) %copy-start.8) | copy-done | bytes 24600
  8.7 0.0 copy-start.9
  8.7 0.7 %copy-done.9 = s32[1,5]{1,0:T(1,128)S(1)} copy-done((s32[1,5]{1,0:T(1,128)S(1)}, s32[1,5]{1,0:T(1,128)}, u32[]{:S(2)}) %copy-start.9) | copy-done | bytes 44
  9.3 43.6 %linked_attention.1 = (bf16[160,1536]{1,0:T(8,128)(2,1)S(1)}, bf16[16,1536]{1,0:T(8,128)(2,1)S(1)}, bf16[160,1536]{1,0:T(8,128)(2,1)S(1)}, bf16[160,1536]{1,0:T(...) custom-call(bf16[160,1536]{1,0:T(8,128)(2,1)S(1)} %copy-done, ...), custom_call_target="tpu_custom_call" | custom-call | tf_op jit(solution)/shard_map/linked_attention/pallas_call | solution.py:401
  52.9 0.8 %copy.26 = bf16[160,1536]{1,0:T(8,128)(2,1)} copy(bf16[160,1536]{1,0:T(8,128)(2,1)S(1)} %get-tuple-element.16) | data formatting | bytes 983040
  53.7 0.6 %copy.27 = bf16[16,1536]{1,0:T(8,128)(2,1)} copy(bf16[16,1536]{1,0:T(8,128)(2,1)S(1)} %get-tuple-element.17) | data formatting | bytes 98304
  54.3 0.8 %copy.28 = bf16[160,1536]{1,0:T(8,128)(2,1)} copy(bf16[160,1536]{1,0:T(8,128)(2,1)S(1)} %get-tuple-element.18) | data formatting | bytes 983040
  55.1 0.8 %copy.29 = bf16[160,1536]{1,0:T(8,128)(2,1)} copy(bf16[160,1536]{1,0:T(8,128)(2,1)S(1)} %get-tuple-element.19) | data formatting | bytes 983040
  55.9 0.8 %copy.30 = bf16[160,1536]{1,0:T(8,128)(2,1)} copy(bf16[160,1536]{1,0:T(8,128)(2,1)S(1)} %get-tuple-element.20) | data formatting | bytes 983040
  56.7 0.6 %copy.31 = bf16[16,1536]{1,0:T(8,128)(2,1)} copy(bf16[16,1536]{1,0:T(8,128)(2,1)S(1)} %get-tuple-element.21) | data formatting | bytes 98304
  57.3 0.6 %copy.32 = bf16[16,1536]{1,0:T(8,128)(2,1)} copy(bf16[16,1536]{1,0:T(8,128)(2,1)S(1)} %get-tuple-element.22) | data formatting | bytes 98304
  57.9 0.6 %copy.33 = bf16[16,1536]{1,0:T(8,128)(2,1)} copy(bf16[16,1536]{1,0:T(8,128)(2,1)S(1)} %get-tuple-element.23) | data formatting | bytes 98304
Async XLA Ops:
  0.6 1.0 %copy-start = (bf16[160,1536]{1,0:T(8,128)(2,1)S(1)}, bf16[160,1536]{1,0:T(8,128)(2,1)}, u32[]{:S(2)}) copy-start(bf16[160,1536]{1,0:T(8,128)(2,1)} %vq.1) | copy-start | bytes 1474564
  1.7 1.0 %copy-start.1 = (bf16[160,1536]{1,0:T(8,128)(2,1)S(1)}, bf16[160,1536]{1,0:T(8,128)(2,1)}, u32[]{:S(2)}) copy-start(bf16[160,1536]{1,0:T(8,128)(2,1)} %vk.1) | copy-start | bytes 1474564
  2.7 1.0 %copy-start.2 = (bf16[160,1536]{1,0:T(8,128)(2,1)S(1)}, bf16[160,1536]{1,0:T(8,128)(2,1)}, u32[]{:S(2)}) copy-start(bf16[160,1536]{1,0:T(8,128)(2,1)} %vv.1) | copy-start | bytes 1474564
  3.7 1.0 %copy-start.3 = (bf16[160,1536]{1,0:T(8,128)(2,1)S(1)}, bf16[160,1536]{1,0:T(8,128)(2,1)}, u32[]{:S(2)}) copy-start(bf16[160,1536]{1,0:T(8,128)(2,1)} %vdo.1) | copy-start | bytes 1474564
  4.8 0.8 %copy-start.4 = (bf16[16,1536]{1,0:T(8,128)(2,1)S(1)}, bf16[16,1536]{1,0:T(8,128)(2,1)}, u32[]{:S(2)}) copy-start(bf16[16,1536]{1,0:T(8,128)(2,1)} %aq.1) | copy-start | bytes 147460
  5.6 0.8 %copy-start.5 = (bf16[16,1536]{1,0:T(8,128)(2,1)S(1)}, bf16[16,1536]{1,0:T(8,128)(2,1)}, u32[]{:S(2)}) copy-start(bf16[16,1536]{1,0:T(8,128)(2,1)} %ak.1) | copy-start | bytes 147460
  6.4 0.8 %copy-start.6 = (bf16[16,1536]{1,0:T(8,128)(2,1)S(1)}, bf16[16,1536]{1,0:T(8,128)(2,1)}, u32[]{:S(2)}) copy-start(bf16[16,1536]{1,0:T(8,128)(2,1)} %av.1) | copy-start | bytes 147460
  7.2 0.8 %copy-start.7 = (bf16[16,1536]{1,0:T(8,128)(2,1)S(1)}, bf16[16,1536]{1,0:T(8,128)(2,1)}, u32[]{:S(2)}) copy-start(bf16[16,1536]{1,0:T(8,128)(2,1)} %ado.1) | copy-start | bytes 147460
  8.0 0.7 %copy-start.8 = (f32[4,1536]{1,0:T(4,128)S(1)}, f32[4,1536]{1,0:T(4,128)}, u32[]{:S(2)}) copy-start(f32[4,1536]{1,0:T(4,128)} %gain.1) | copy-start | bytes 73732
  8.7 0.7 %copy-start.9 = (s32[1,5]{1,0:T(1,128)S(1)}, s32[1,5]{1,0:T(1,128)}, u32[]{:S(2)}) copy-start(s32[1,5]{1,0:T(1,128)} %link.1) | copy-start | bytes 64

commit v2 on v1

--- a/solution.py
+++ b/solution.py
@@ -66,15 +66,29 @@
 
 
 def kernel(
-    along, count, vq, vk, vv, aq, ak, av, gain, vdo, ado, link,
+    along, count, h_vq, h_vk, h_vv, h_aq, h_ak, h_av, h_gain, h_vdo, h_ado, h_link,
     o_v, o_a, g_vq, g_vk, g_vv, g_aq, g_ak, g_av,
     win, po, po_in, gr, gr_in, stat, qv, kv, ea, dpa, pab, gab, rq, rk, tab_v, tab_a, coef, bias, wts,
+    vq, vk, vv, aq, ak, gain, vdo, link, s_in,
     s_win, r_win, s_stat, r_stat, s_po, r_po, s_gr, r_gr,
 ):
     vrows, hd = vq.shape
     arows = aq.shape[0]
     heads = hd // DH
     wrows = SPAN * arows
+    own = pl.ds(R * arows, arows)
+    loads = [
+        pltpu.make_async_copy(src, dst, s_in.at[i])
+        for i, (src, dst) in enumerate(
+            (
+                (h_aq, aq), (h_ak, ak), (h_gain, gain),
+                (h_ado, win.at[AUDIO_DOUT, own]), (h_av, win.at[AUDIO_V, own]),
+                (h_vk, vk), (h_vq, vq), (h_vv, vv), (h_vdo, vdo), (h_link, link),
+            )
+        )
+    ]
+    for load in loads:
+        load.start()
     clip = lax.axis_index("clips")
     me = lax.axis_index("video") * along + lax.axis_index("audio")
 
@@ -108,6 +122,9 @@
     c, s = tables(vplace.astype(f32))
     tab_v[0], tab_v[1] = c, s
 
+    for load in loads[:3]:
+        load.wait()
+
     def audio_prepare(h, _):
         hs = lanes(h)
         for src, slot, g in ((aq, AUDIO_Q, 2), (ak, AUDIO_K, 3)):
@@ -116,9 +133,9 @@
             win[slot, rows(R), hs] = y.astype(bf16)
         return 0
 
-    lax.fori_loop(0, heads, audio_prepare, 0)
-    win[AUDIO_DOUT, rows(R), :] = ado[...]
-    win[AUDIO_V, rows(R), :] = av[...]
+    lax.fori_loop(0, heads, audio_prepare, 0, unroll=4)
+    for load in loads[3:5]:
+        load.wait()
 
     pl.semaphore_wait(barrier, jnp.minimum(me, REACH) + jnp.minimum(count - 1 - me, REACH))
 
@@ -203,6 +220,8 @@
         def _():
             stat[REACH - d] = empty
 
+    for load in loads[5:]:
+        load.wait()
     lane_slot = lax.broadcasted_iota(jnp.int32, (1, wrows), 1) // arows
     linked_row = jnp.zeros((1, wrows), jnp.int32)
     for j in range(SPAN):
@@ -221,7 +240,7 @@
             dst[:, hs] = y.astype(bf16)
         return 0
 
-    lax.fori_loop(0, heads, video_prepare, 0)
+    lax.fori_loop(0, heads, video_prepare, 0, unroll=4)
 
     win_each((AUDIO_Q, AUDIO_DOUT), "wait_recv")
 
@@ -244,7 +263,7 @@
         po[:, hs] = tn(e.astype(bf16), v).astype(bf16)
         return 0
 
-    lax.fori_loop(0, heads, audio_forward, 0)
+    lax.fori_loop(0, heads, audio_forward, 0, unroll=4)
     stat_each("start")
     back_each(po, po_in, s_po, r_po, "start")
 
@@ -271,7 +290,7 @@
         ).astype(bf16)
         return 0
 
-    lax.fori_loop(0, heads, video_side, 0)
+    lax.fori_loop(0, heads, video_side, 0, unroll=4)
     for member in (D_KEY, D_VALUE):
         back_each(gr.at[member], gr_in.at[member], s_gr.at[member], r_gr.at[member], "start")
 
@@ -307,7 +326,7 @@
         gr[D_QUERY, :, hs] = (tn(ga, kv[:, hs]) * SCALE).astype(bf16)
         return 0
 
-    lax.fori_loop(0, heads, audio_back, 0)
+    lax.fori_loop(0, heads, audio_back, 0, unroll=4)
     back_each(gr.at[D_QUERY], gr_in.at[D_QUERY], s_gr.at[D_QUERY], r_gr.at[D_QUERY], "start")
 
     def video_back(h, _):
@@ -319,7 +338,7 @@
         ).astype(bf16)
         return 0
 
-    lax.fori_loop(0, heads, video_back, 0)
+    lax.fori_loop(0, heads, video_back, 0, unroll=4)
 
     turned = jnp.transpose(wts[...])[R * arows : (R + 1) * arows, :]
     back_each(po, po_in, s_po, r_po, "wait_recv")
@@ -346,7 +365,7 @@
             ).astype(bf16)
             return 0
 
-        lax.fori_loop(0, heads, body, 0)
+        lax.fori_loop(0, heads, body, 0, unroll=4)
 
     for member in (D_KEY, D_VALUE):
         back_each(gr.at[member], gr_in.at[member], s_gr.at[member], r_gr.at[member], "wait_recv")
@@ -360,6 +379,16 @@
     back_each(po, po_in, s_po, r_po, "wait_send")
     for member in range(3):
         back_each(gr.at[member], gr_in.at[member], s_gr.at[member], r_gr.at[member], "wait_send")
+
+
+def write_out(*refs):
+    n = len(refs) // 2
+    sems = refs[-1]
+    copies = [pltpu.make_async_copy(refs[i], refs[n + i], sems.at[i]) for i in range(n)]
+    for copy in copies:
+        copy.start()
+    for copy in copies:
+        copy.wait()
 
 
 def on_device(along, count, *args):
@@ -393,22 +422,39 @@
         pltpu.VMEM((2, 16, DH), f32),
         pltpu.VMEM((wrows, vrows), f32),
         pltpu.VMEM((DH, DH), f32),
+        pltpu.VMEM((vrows, hd), bf16),
+        pltpu.VMEM((vrows, hd), bf16),
+        pltpu.VMEM((vrows, hd), bf16),
+        pltpu.VMEM((arows, hd), bf16),
+        pltpu.VMEM((arows, hd), bf16),
+        pltpu.VMEM(args[6].shape, f32),
+        pltpu.VMEM((vrows, hd), bf16),
+        pltpu.SMEM(args[9].shape, jnp.int32),
+        dma((10,)),
         dma((4, n)), dma((4, n)),
         dma((2 * REACH,)), dma((2 * REACH,)),
         dma((n,)), dma((n,)),
         dma((3, n)), dma((3, n)),
     ]
-    return pl.pallas_call(
+    results = pl.pallas_call(
         functools.partial(kernel, along, count),
         out_shape=[video, audio, video, video, video, audio, audio, audio],
-        in_specs=[vmem] * 9 + [pl.BlockSpec(memory_space=pltpu.SMEM)],
+        in_specs=[pl.BlockSpec(memory_space=pl.ANY)] * 10,
         out_specs=[vmem] * 8,
         scratch_shapes=scratch,
         compiler_params=pltpu.CompilerParams(
-            collective_id=0, has_side_effects=True, vmem_limit_bytes=40 * 1024 * 1024
+            collective_id=0, has_side_effects=True, vmem_limit_bytes=56 * 1024 * 1024
         ),
         name="linked_attention",
     )(*args)
+    return pl.pallas_call(
+        write_out,
+        out_shape=[video, audio, video, video, video, audio, audio, audio],
+        in_specs=[vmem] * 8,
+        out_specs=[pl.BlockSpec(memory_space=pl.ANY)] * 8,
+        scratch_shapes=[dma((8,))],
+        name="write_out",
+    )(*results)
 
 
 def solution(mesh):

time: 59.1 us -> 40.1 us (0.68)
  local copies, waits for them, and re-layouts: 14.3 us -> 0 us
  Pallas kernels: 43.6 us -> 39 us
    unnamed x28 -> x0, local copies, waits for them, and re-layouts: 14.3 us -> none
    pallas_call x1, Pallas kernels: 43.6 us -> 36.1 us  [on_device(): pl.pallas_call(functools.partial(kernel, along, count), out_shape=[video,...]
    pallas_call x0 -> x1, Pallas kernels: none -> 2.91 us  [on_device(): pl.pallas_call(write_out, out_shape=[video, audio, video, video, video, a...]
where the time goes in v2:
time: 40.1 us; the launch traced here: 39.7 us
  Pallas kernels  39 us (97%)
  between operations  0.64 us (2%)
    pallas_call x1, Pallas kernels, on_device(): pl.pallas_call(functools.partial(kernel, along, count), out_shape=[video,...  36.1 us
    pallas_call x1, Pallas kernels, on_device(): pl.pallas_call(write_out, out_shape=[video, audio, video, video, video, a...  2.91 us

profile of v2, /device:TPU:15, one launch (start us, length us, event | category | flops | bytes accessed | tf_op | source)
XLA Modules:
  0.0 39.7 jit_solution(16800432950203353382)
XLA Ops:
  0.6 36.1 %linked_attention.1 = (bf16[160,1536]{1,0:T(8,128)(2,1)}, bf16[16,1536]{1,0:T(8,128)(2,1)}, bf16[160,1536]{1,0:T(8,128)(2,1)}, bf16[160,1536]{1,0:T(8,128)(2,1)}...) custom-call(bf16[160,1536]{1,0:T(8,128)(2,1)} %h_vq.1, ...), custom_call_target="tpu_custom_call" | custom-call | tf_op jit(solution)/shard_map/linked_attention/pallas_call | solution.py:439
  36.8 2.9 %write_out.1 = (bf16[160,1536]{1,0:T(8,128)(2,1)}, bf16[16,1536]{1,0:T(8,128)(2,1)}, bf16[160,1536]{1,0:T(8,128)(2,1)}, bf16[160,1536]{1,0:T(8,128)(2,1)}, bf16[...) custom-call(bf16[160,1536]{1,0:T(8,128)(2,1)} %get-tuple-element.16.refs_0, ...), custom_call_target="tpu_custom_call" | custom-call | tf_op jit(solution)/shard_map/write_out/pallas_call | solution.py:450

commit v3 on v2

--- a/solution.py
+++ b/solution.py
@@ -172,14 +172,44 @@
             device_id_type=pl.DeviceIdType.MESH,
         )
 
-    def win_each(members, action):
+    even = lax.rem(me, 2) == 0
+
+    def win_each(members, action, slots=range(len(SLOTS))):
         for member in members:
-            for n, j in enumerate(SLOTS):
+            for n in slots:
+                j = SLOTS[n]
                 other = me + j - R if action == "wait_recv" else me + R - j
-
-                @pl.when(valid(other))
+                go = valid(other)
+                if action != "wait_recv" and j == 0:
+                    go = jnp.logical_and(go, even)
+                if action != "wait_recv" and j == SPAN - 1:
+                    go = jnp.logical_and(go, jnp.logical_not(even))
+
+                @pl.when(go)
                 def _():
                     getattr(win_copy(member, n, other), action)()
+
+    def pass_on(members, action):
+        for member in members:
+            for parity, near, n, spare, step in ((0, 1, 0, 3, 1), (1, 3, 3, 0, -1)):
+                go = jnp.logical_and(valid(me - step), valid(me + step))
+
+                @pl.when(jnp.logical_and(go, lax.rem(me, 2) == parity))
+                def _():
+                    copy = pltpu.make_async_remote_copy(
+                        src_ref=win.at[member, rows(near)],
+                        dst_ref=win.at[member, rows(SLOTS[n])],
+                        send_sem=s_win.at[member, spare],
+                        recv_sem=r_win.at[member, n],
+                        device_id=device(me + step),
+                        device_id_type=pl.DeviceIdType.MESH,
+                    )
+                    getattr(copy, action)()
+
+    def win_arrive(members):
+        win_each(members, "wait_recv", (1, 2))
+        pass_on(members, "start")
+        win_each(members, "wait_recv", (0, 3))
 
     def back_each(src, dst, send, recv, action):
         for n, j in enumerate(SLOTS):
@@ -242,7 +272,7 @@
 
     lax.fori_loop(0, heads, video_prepare, 0, unroll=4)
 
-    win_each((AUDIO_Q, AUDIO_DOUT), "wait_recv")
+    win_arrive((AUDIO_Q, AUDIO_DOUT))
 
     def audio_forward(h, _):
         hs = lanes(h)
@@ -267,7 +297,7 @@
     stat_each("start")
     back_each(po, po_in, s_po, r_po, "start")
 
-    win_each((AUDIO_K, AUDIO_V), "wait_recv")
+    win_arrive((AUDIO_K, AUDIO_V))
 
     def video_side(h, _):
         hs = lanes(h)
@@ -375,6 +405,7 @@
     audio_grad(aq, D_QUERY, 2, g_aq)
 
     win_each(range(4), "wait_send")
+    pass_on(range(4), "wait_send")
     stat_each("wait_send")
     back_each(po, po_in, s_po, r_po, "wait_send")
     for member in range(3):

time: 40.1 us -> 38.3 us (0.955)
  Pallas kernels: 39 us -> 37.2 us
    pallas_call x1, Pallas kernels: 36.1 us -> 34.3 us  [on_device(): pl.pallas_call(functools.partial(kernel, along, count), out_shape=[video,...]
where the time goes in v3:
time: 38.3 us; the launch traced here: 37.9 us
  Pallas kernels  37.2 us (97%)
  between operations  0.64 us (2%)
    pallas_call x1, Pallas kernels, on_device(): pl.pallas_call(functools.partial(kernel, along, count), out_shape=[video,...  34.3 us
    pallas_call x1, Pallas kernels, on_device(): pl.pallas_call(write_out, out_shape=[video, audio, video, video, video, a...  2.91 us

profile of v3, /device:TPU:15, one launch (start us, length us, event | category | flops | bytes accessed | tf_op | source)
XLA Modules:
  0.0 37.9 jit_solution(18428504220037089108)
XLA Ops:
  0.6 34.3 %linked_attention.1 = (bf16[160,1536]{1,0:T(8,128)(2,1)}, bf16[16,1536]{1,0:T(8,128)(2,1)}, bf16[160,1536]{1,0:T(8,128)(2,1)}, bf16[160,1536]{1,0:T(8,128)(2,1)}...) custom-call(bf16[160,1536]{1,0:T(8,128)(2,1)} %h_vq.1, ...), custom_call_target="tpu_custom_call" | custom-call | tf_op jit(solution)/shard_map/linked_attention/pallas_call | solution.py:470
  35.0 2.9 %write_out.1 = (bf16[160,1536]{1,0:T(8,128)(2,1)}, bf16[16,1536]{1,0:T(8,128)(2,1)}, bf16[160,1536]{1,0:T(8,128)(2,1)}, bf16[160,1536]{1,0:T(8,128)(2,1)}, bf16[...) custom-call(bf16[160,1536]{1,0:T(8,128)(2,1)} %get-tuple-element.16.refs_0, ...), custom_call_target="tpu_custom_call" | custom-call | tf_op jit(solution)/shard_map/write_out/pallas_call | solution.py:481

commit v4 on v3

--- a/solution.py
+++ b/solution.py
@@ -70,7 +70,7 @@
     o_v, o_a, g_vq, g_vk, g_vv, g_aq, g_ak, g_av,
     win, po, po_in, gr, gr_in, stat, qv, kv, ea, dpa, pab, gab, rq, rk, tab_v, tab_a, coef, bias, wts,
     vq, vk, vv, aq, ak, gain, vdo, link, s_in,
-    s_win, r_win, s_stat, r_stat, s_po, r_po, s_gr, r_gr,
+    s_win, r_win, s_stat, r_stat, s_po, r_po, s_gr, r_gr, hand, s_hand, r_hand,
 ):
     vrows, hd = vq.shape
     arows = aq.shape[0]
@@ -219,6 +219,47 @@
             def _():
                 getattr(back_copy(src, dst, send, recv, n, other), action)()
 
+    def gr_each(members, action, merged=None):
+        for member in members:
+            for n, j in enumerate(SLOTS):
+                other = me + R - j if action == "wait_recv" else me + j - R
+                for parity in (0, 1):
+                    if j == 0 and parity or j == SPAN - 1 and not parity:
+                        continue
+                    if merged is not None and merged != ((j, parity) in ((1, 0), (3, 1))):
+                        continue
+
+                    @pl.when(jnp.logical_and(valid(other), lax.rem(me, 2) == parity))
+                    def _():
+                        copy = back_copy(
+                            gr.at[member], gr_in.at[member], s_gr.at[member], r_gr.at[member], n, other
+                        )
+                        getattr(copy, action)()
+
+    def hand_each(members, action):
+        for member in members:
+            for parity, j, step in ((0, SPAN - 1, 1), (1, 0, -1)):
+                if action == "wait_recv":
+                    go = jnp.logical_and(valid(me + step), valid(me - step))
+                else:
+                    go = jnp.logical_and(valid(me + 2 * step), valid(me + step))
+
+                @pl.when(jnp.logical_and(go, lax.rem(me, 2) == parity))
+                def _():
+                    copy = pltpu.make_async_remote_copy(
+                        src_ref=gr.at[member, rows(j)],
+                        dst_ref=hand.at[member],
+                        send_sem=s_hand.at[member],
+                        recv_sem=r_hand.at[member],
+                        device_id=device(me + step),
+                        device_id_type=pl.DeviceIdType.MESH,
+                    )
+                    getattr(copy, action)()
+                    if action == "wait_recv":
+                        near = rows(1 if parity == 0 else 3)
+                        both = gr[member, near, :].astype(f32) + hand[member].astype(f32)
+                        gr[member, near, :] = both.astype(bf16)
+
     def stat_each(action):
         for d in others:
             other = me - d if action == "wait_recv" else me + d
@@ -239,6 +280,13 @@
         @pl.when(jnp.logical_not(valid(me + R - j)))
         def _():
             po_in[rows(j), :] = jnp.zeros((arows, hd), bf16)
+            for member in range(3):
+                gr_in[member, rows(j), :] = jnp.zeros((arows, hd), bf16)
+
+    for parity, j in ((0, SPAN - 1), (1, 0)):
+
+        @pl.when(lax.rem(me, 2) == parity)
+        def _():
             for member in range(3):
                 gr_in[member, rows(j), :] = jnp.zeros((arows, hd), bf16)
 
@@ -321,9 +369,11 @@
         return 0
 
     lax.fori_loop(0, heads, video_side, 0, unroll=4)
-    for member in (D_KEY, D_VALUE):
-        back_each(gr.at[member], gr_in.at[member], s_gr.at[member], r_gr.at[member], "start")
-
+    hand_each((D_KEY, D_VALUE), "start")
+    gr_each((D_KEY, D_VALUE), "start", merged=False)
+
+    hand_each((D_KEY, D_VALUE), "wait_recv")
+    gr_each((D_KEY, D_VALUE), "start", merged=True)
     stat_each("wait_recv")
     lane = lax.broadcasted_iota(jnp.int32, (16, DH), 1)
     tops, totals, dots = [], [], []
@@ -357,7 +407,8 @@
         return 0
 
     lax.fori_loop(0, heads, audio_back, 0, unroll=4)
-    back_each(gr.at[D_QUERY], gr_in.at[D_QUERY], s_gr.at[D_QUERY], r_gr.at[D_QUERY], "start")
+    hand_each((D_QUERY,), "start")
+    gr_each((D_QUERY,), "start", merged=False)
 
     def video_back(h, _):
         hs = lanes(h)
@@ -368,7 +419,10 @@
         ).astype(bf16)
         return 0
 
-    lax.fori_loop(0, heads, video_back, 0, unroll=4)
+    lax.fori_loop(0, heads // 3, video_back, 0, unroll=4)
+    hand_each((D_QUERY,), "wait_recv")
+    gr_each((D_QUERY,), "start", merged=True)
+    lax.fori_loop(heads // 3, heads, video_back, 0, unroll=4)
 
     turned = jnp.transpose(wts[...])[R * arows : (R + 1) * arows, :]
     back_each(po, po_in, s_po, r_po, "wait_recv")
@@ -397,19 +451,18 @@
 
         lax.fori_loop(0, heads, body, 0, unroll=4)
 
-    for member in (D_KEY, D_VALUE):
-        back_each(gr.at[member], gr_in.at[member], s_gr.at[member], r_gr.at[member], "wait_recv")
+    gr_each((D_KEY, D_VALUE), "wait_recv")
     g_av[...] = merged(D_VALUE, slice(None)).astype(bf16)
     audio_grad(ak, D_KEY, 3, g_ak)
-    back_each(gr.at[D_QUERY], gr_in.at[D_QUERY], s_gr.at[D_QUERY], r_gr.at[D_QUERY], "wait_recv")
+    gr_each((D_QUERY,), "wait_recv")
     audio_grad(aq, D_QUERY, 2, g_aq)
 
     win_each(range(4), "wait_send")
     pass_on(range(4), "wait_send")
     stat_each("wait_send")
     back_each(po, po_in, s_po, r_po, "wait_send")
-    for member in range(3):
-        back_each(gr.at[member], gr_in.at[member], s_gr.at[member], r_gr.at[member], "wait_send")
+    hand_each(range(3), "wait_send")
+    gr_each(range(3), "wait_send")
 
 
 def write_out(*refs):
@@ -466,6 +519,8 @@
         dma((2 * REACH,)), dma((2 * REACH,)),
         dma((n,)), dma((n,)),
         dma((3, n)), dma((3, n)),
+        pltpu.VMEM((3, arows, hd), bf16),
+        dma((3,)), dma((3,)),
     ]
     results = pl.pallas_call(
         functools.partial(kernel, along, count),

time: 38.3 us -> 35.6 us (0.930)
  Pallas kernels: 37.2 us -> 34.3 us
    pallas_call x1, Pallas kernels: 34.3 us -> 31.4 us  [on_device(): pl.pallas_call(functools.partial(kernel, along, count), out_shape=[video,...]
where the time goes in v4:
time: 35.6 us; the launch traced here: 34.9 us
  Pallas kernels  34.3 us (96%)
  between operations  0.64 us (2%)
    pallas_call x1, Pallas kernels, on_device(): pl.pallas_call(functools.partial(kernel, along, count), out_shape=[video,...  31.4 us
    pallas_call x1, Pallas kernels, on_device(): pl.pallas_call(write_out, out_shape=[video, audio, video, video, video, a...  2.91 us

profile of v4, /device:TPU:15, one launch (start us, length us, event | category | flops | bytes accessed | tf_op | source)
XLA Modules:
  0.0 34.9 jit_solution(9109802164729983889)
XLA Ops:
  0.6 31.4 %linked_attention.1 = (bf16[160,1536]{1,0:T(8,128)(2,1)}, bf16[16,1536]{1,0:T(8,128)(2,1)}, bf16[160,1536]{1,0:T(8,128)(2,1)}, bf16[160,1536]{1,0:T(8,128)(2,1)}...) custom-call(bf16[160,1536]{1,0:T(8,128)(2,1)} %h_vq.1, ...), custom_call_target="tpu_custom_call" | custom-call | tf_op jit(solution)/shard_map/linked_attention/pallas_call | solution.py:525
  32.0 2.9 %write_out.1 = (bf16[160,1536]{1,0:T(8,128)(2,1)}, bf16[16,1536]{1,0:T(8,128)(2,1)}, bf16[160,1536]{1,0:T(8,128)(2,1)}, bf16[160,1536]{1,0:T(8,128)(2,1)}, bf16[...) custom-call(bf16[160,1536]{1,0:T(8,128)(2,1)} %get-tuple-element.16.refs_0, ...), custom_call_target="tpu_custom_call" | custom-call | tf_op jit(solution)/shard_map/write_out/pallas_call | solution.py:536
